TPU v7x, 256 devices: a whole 4x4x8 slice. The times are simulated.
256 devices in a mesh: feat: 64 (over x, z, core), grp: 4 (over y).
Axes of the slice: x: 4, y: 4, z: 8, core: 2. Of those that a mesh axis runs over, the one named last changes fastest.
Arguments:
- features: bfloat16 [4, 4096, 8192], P('grp', 'feat'), may hold values from -6 to 6
- nbr_one: int32 [4, 10, 8192], P('grp'), may hold values from 0 to 8191
- w_one: bfloat16 [2, 4096, 512], P(None, 'feat'), may hold values from -0.09375 to 0.09375
- b_one: float32 [512], replicated, may hold values from -3 to 3
- send_rows: int32 [4, 64, 64, 4, 2], P('grp', 'feat'), may hold values from 0 to 127
- nbr_slot: int32 [4, 25, 8192], P('grp', None, 'feat'), may hold values from 0 to 511
- degree: int32 [4, 8192], P('grp', 'feat'), may hold values from 1 to 25
- w_two: bfloat16 [1024, 512], replicated, may hold values from -0.25 to 0.25
- cotangent: bfloat16 [4, 8192, 512], P('grp', 'feat'), may hold values from -6 to 6
Outputs:
- embedding: bfloat16 [4, 8192, 512], P('grp', 'feat')
- grad_w_one: float32 [2, 4096, 512], P(None, 'feat')
- grad_b_one: float32 [512], replicated
- grad_w_two: float32 [1024, 512], P(('feat', 'grp'))
Inputs may be any that keep to these rules, and one draw needn't show every extreme that they name: `send_rows`: rows local to the owning device. Slots at or past degree are unused.
All inputs are finite; a program needn't handle non-finite values.
Results may differ from a plain program's by a relative error of at most 0.019.
The roundings to bfloat16 on the way count: a program that leaves them out, or rounds other values in their place, can miss the bound.
Values may be sent and summed in bfloat16 or wider, within the bound.
No kernel may reach another device: no remote copies, remote signals or barrier semaphores. Data moves between devices by JAX's collectives and lax.ppermute only.
A program may use at most 128 MiB of HBM per device.

v0:
```python
import jax
import jax.numpy as jnp
from jax import lax
from jax.sharding import PartitionSpec as P


def contract_rows(left, right):
    return lax.dot_general(
        left, right, (((0,), (0,)), ((), ())), preferred_element_type=jnp.float32
    )


def on_device(features, nbr_one, w_one, b_one, send_rows, nbr_slot, degree, w_two, cotangent):
    local_feats = features[0]
    neighbours = nbr_one[0]
    width = w_two.shape[1]
    feat_devices = lax.axis_size("feat")
    group_nodes = local_feats.shape[1]
    feat_rows_local = local_feats.shape[0]
    owned = group_nodes // feat_devices
    fanout = neighbours.shape[0]
    node_major = local_feats.T
    picked_rows = jnp.take(node_major, neighbours.reshape(-1), axis=0)
    summed = jnp.sum(
        picked_rows.reshape(fanout, group_nodes, feat_rows_local).astype(jnp.float32), axis=0
    )
    agg_local = (summed / fanout).T.astype(jnp.bfloat16)
    feat_rows = local_feats
    agg_rows = agg_local
    pre_one = lax.psum_scatter(
        contract_rows(feat_rows, w_one[0]) + contract_rows(agg_rows, w_one[1]),
        "feat",
        scatter_dimension=0,
        tiled=True,
    )
    pre_one = pre_one + b_one
    h_one = jnp.maximum(pre_one, 0.0).astype(jnp.bfloat16)
    send_list = send_rows[0, 0]
    outgoing = h_one[send_list]
    received = lax.all_to_all(
        lax.all_to_all(outgoing, "feat", split_axis=0, concat_axis=0, tiled=True),
        "grp",
        split_axis=1,
        concat_axis=1,
        tiled=True,
    )
    flat_table = received.reshape(-1, width)
    slot_index = nbr_slot[0]
    degree_row = degree[0]
    live_mask = jnp.arange(slot_index.shape[0], dtype=jnp.int32)[:, None] < degree_row[None, :]
    degree_f = degree_row.astype(jnp.float32)[:, None]
    accum = jnp.zeros((owned, width), jnp.float32)
    for index in range(slot_index.shape[0]):
        picked = flat_table[slot_index[index]].astype(jnp.float32)
        accum = accum + jnp.where(live_mask[index][:, None], picked, 0.0)
    agg_two = (accum / degree_f).astype(jnp.bfloat16)
    embedding = (
        jnp.dot(h_one, w_two[:width], preferred_element_type=jnp.float32)
        + jnp.dot(agg_two, w_two[width:], preferred_element_type=jnp.float32)
    ).astype(jnp.bfloat16)
    cot_rows = cotangent[0]
    two_terms = jnp.concatenate(
        [contract_rows(h_one, cot_rows), contract_rows(agg_two, cot_rows)], axis=0
    )
    grad_w_two = lax.psum_scatter(two_terms, ("feat", "grp"), scatter_dimension=0, tiled=True)
    d_self = jnp.dot(cot_rows, w_two[:width].T, preferred_element_type=jnp.float32)
    d_agg = jnp.dot(cot_rows, w_two[width:].T, preferred_element_type=jnp.float32)
    scaled = d_agg / degree_f
    per_slot = jnp.where(live_mask[:, :, None], scaled[None, :, :], 0.0).reshape(-1, width)
    d_table = jax.ops.segment_sum(
        per_slot, slot_index.reshape(-1), num_segments=flat_table.shape[0]
    )
    returned = lax.all_to_all(
        lax.all_to_all(
            d_table.reshape(received.shape).astype(jnp.bfloat16),
            "feat",
            split_axis=0,
            concat_axis=0,
            tiled=True,
        ),
        "grp",
        split_axis=1,
        concat_axis=1,
        tiled=True,
    ).astype(jnp.float32)
    d_near = jax.ops.segment_sum(
        returned.reshape(-1, width), send_list.reshape(-1), num_segments=owned
    )
    d_pre = jnp.where(pre_one > 0.0, d_self + d_near, 0.0).astype(jnp.bfloat16)
    pieces = lax.all_gather(d_pre, "feat", axis=0, tiled=True)
    feat_rows = local_feats
    agg_rows = agg_local
    grad_self = jnp.dot(feat_rows, pieces, preferred_element_type=jnp.float32)
    grad_near = jnp.dot(agg_rows, pieces, preferred_element_type=jnp.float32)
    bias_part = jnp.sum(pieces.astype(jnp.float32), axis=0)
    grad_w_one, grad_b_one = (
        lax.psum(jnp.stack([grad_self, grad_near], axis=0).astype(jnp.bfloat16), "grp").astype(
            jnp.float32
        ),
        lax.psum(bias_part.astype(jnp.bfloat16), "grp").astype(jnp.float32),
    )
    return (embedding[None], grad_w_one, grad_b_one, grad_w_two)


def solution(mesh):
    return jax.shard_map(
        on_device,
        mesh=mesh,
        in_specs=(
            P("grp", "feat", None),
            P("grp", None, None),
            P(None, "feat", None),
            P(),
            P("grp", "feat", None, None, None),
            P("grp", None, "feat"),
            P("grp", "feat"),
            P(),
            P("grp", "feat", None),
        ),
        out_specs=(P("grp", "feat", None), P(None, "feat", None), P(), P(("feat", "grp"), None)),
        check_vma=False,
    )
```

profile of v0, /device:TPU:2, one launch (start us, length us, event | category | flops | bytes accessed | tf_op | source)
XLA Modules:
  0.0 937.4 jit_solution(18227934692849070402)
XLA Ops:
  7.2 2.1 copy.58
  11.9 9.5 %fusion.5 = f32[8192,512]{1,0:T(8,128)} fusion(bf16[1,64,8192]{2,1,0:T(8,128)(2,1)} %param.9, bf16[2,64,512]{2,1,0:T(8,128)(2,1)} %param.11), kind=kOutput, calls=%fused_computation.45 | convolution fusion | flops 536870912 | bytes 17891328 | tf_op jit(solution)/shard_map/dot_general | solution.py:8
  21.4 286.0 %gather_fusion = bf16[81920,64]{1,0:T(8,128)(2,1)} fusion(bf16[8192,64]{1,0:T(8,128)(2,1)S(1)} %bitcast.208, s32[81920]{0:T(1024)S(1)} %broadcast_clamp_fusion), kind=kCustom, calls=%fused_computation | custom fusion | bytes 21299200 | tf_op jit(solution)/shard_map/jit(_take)/gather | solution.py:23
  307.4 16.3 %convert_reduce_fusion = f32[8192,64]{1,0:T(8,128)S(1)} fusion(bf16[10,8192,64]{2,1,0:T(8,128)(2,1)} %bitcast.209, pred[10,8192]{1,0:T(8,128)(4,1)S(1)} %compare_and_fusion), kind=kLoop, calls=%fused_computation.29 | loop fusion | flops 15204352 | bytes 12664832 | tf_op jit(solution)/shard_map/reduce_sum | solution.py:24
  323.7 2.0 copy-done.2
  325.6 13.9 %convolution_add_fusion = f32[8192,512]{1,0:T(8,128)} fusion(f32[8192,512]{1,0:T(8,128)} %fusion.5, f32[8192,64]{1,0:T(8,128)S(1)} %convert_reduce_fusion, bf16[2,64,512]{2,1,0:T(8,128)(2,1)S(1)} %copy-done.8), kind=kOutput, calls=%fused_computation.30 | convolution fusion | flops 542113792 | bytes 37814272 | tf_op jit(solution)/shard_map/dot_general | solution.py:8
  341.1 3.3 bitcast_select_fusion
  344.4 22.5 %scatter_custom_fusion = f32[512,512]{1,0:T(8,128)S(1)} fusion(s32[3200]{0:T(1024)S(1)} %bitcast.212, f32[3200,512]{1,0:T(8,128)} %bitcast_select_fusion, f32[]{:T(128)} %constant.13.clone.1), kind=kCustom, calls=%fused_computation.48 | custom fusion | flops 1638400 | bytes 1049088 | tf_op jit(solution)/shard_map/scatter-add | solution.py:70
  367.2 28.5 %all_to_all.20 = bf16[64,4,2,512]{3,2,1,0:T(2,128)(2,1)S(1)} all-to-all(bf16[64,4,2,512]{3,2,1,0:T(2,128)(2,1)S(1)} %convert_element_type.149), channel_id=1, replica_groups=mesh['feat'=64,'grp'=4] {'feat'}, dimensions={0} | all-to-all | bytes 1048576 | tf_op jit(solution)/shard_map/all_to_all | solution.py:74
  396.9 4.5 all-to-all-start.3
  402.5 9.1 all-to-all-done.3
  413.3 3.8 scatter_fusion
  417.2 114.0 %reduce-scatter.2.cloned.1.call-done = f32[128,512]{1,0:T(8,128)} async-done(((f32[8192,512]{1,0:T(8,128)}), f32[128,512]{1,0:T(8,128)}) %reduce-scatter.2.cloned.1.call-update) | async-done | bytes 262160 | tf_op jit(solution)/shard_map/reduce_scatter | solution.py:30
  534.3 2.0 gather_fusion.1
  537.3 8.4 all-to-all-start
  547.1 18.6 %all-to-all-done = bf16[64,4,2,512]{3,2,1,0:T(2,128)(2,1)S(1)} async-done(((bf16[64,4,2,512]{3,2,1,0:T(2,128)(2,1)}), bf16[64,4,2,512]{3,2,1,0:T(2,128)(2,1)S(1)}, u32[]{:S(2)}, u32[]{:S(2)}) %all-to-all-start) | async-done | bytes 524320 | tf_op jit(solution)/shard_map/all_to_all | solution.py:41
  566.9 4.3 all-to-all-start.1
  572.5 8.6 all-to-all-done.1
  615.9 2.5 divide_convert_fusion
  620.6 5.1 fusion.3
  630.8 251.3 %all-reduce.6.cloned.1.call-done = f32[1024,512]{1,0:T(8,128)} async-done(((f32[1024,512]{1,0:T(8,128)}), f32[1024,512]{1,0:T(8,128)}) %all-reduce.6.cloned.1.call-update) | async-done | bytes 2097168
  883.3 4.5 reduce_sum.22
  887.9 10.1 %psum.15 = bf16[512]{0:T(512)(128)(2,1)S(1)} all-reduce(bf16[512]{0:T(512)(128)(2,1)S(1)} %reduce_sum.22), channel_id=1, replica_groups=mesh['feat'=64,'grp'=4] {'grp'}, use_global_device_ids=true, to_apply=%region_6.7 | all-reduce | flops 512 | bytes 2048 | tf_op jit(solution)/shard_map/psum | solution.py:100
  898.6 30.6 %all-reduce.4.cloned.1.call-done = bf16[2,64,512]{2,1,0:T(8,128)(2,1)} async-done(((bf16[2,64,512]{2,1,0:T(8,128)(2,1)}), bf16[2,64,512]{2,1,0:T(8,128)(2,1)}) %all-reduce.4.cloned.1.call-update) | async-done | bytes 131088 | tf_op jit(solution)/shard_map/psum | solution.py:97
  (120 shorter events, 61.8 us)
Async XLA Ops:
  7.2 333.1 %copy-start = (bf16[1,128,512]{2,1,0:T(8,128)(2,1)S(1)}, bf16[1,128,512]{2,1,0:T(8,128)(2,1)}, u32[]{:S(2)}) copy-start(bf16[1,128,512]{2,1,0:T(8,128)(2,1)} %param.17) | copy-start | bytes 393220
  7.2 524.0 %reduce-scatter.2.cloned.1.call-start = ((), (), s32[]{:S(2)}) async-start(), calls=%async_computation.5 | async-start | bytes 17039360 | tf_op jit(solution)/shard_map/reduce_scatter | solution.py:30
  307.4 18.2 %copy-start.8 = (bf16[2,64,512]{2,1,0:T(8,128)(2,1)S(1)}, bf16[2,64,512]{2,1,0:T(8,128)(2,1)}, u32[]{:S(2)}) copy-start(bf16[2,64,512]{2,1,0:T(8,128)(2,1)} %param.11) | copy-start | bytes 393220
  323.6 2.0 copy-start.2
  339.6 0.7 copy-start.13
  339.6 1.2 copy-start.5
  339.6 4.8 copy-start.9
  340.3 4.2 copy-start.15
  341.1 60.2 %copy-start.10 = (s32[1,1,64,4,2]{2,4,3,1,0:T(2,128)S(1)}, s32[1,1,64,4,2]{2,4,3,1,0:T(2,128)}, u32[]{:S(2)}) copy-start(s32[1,1,64,4,2]{2,4,3,1,0:T(2,128)} %param.13) | copy-start | bytes 6148
  396.9 14.7 %all-to-all-start.3 = ((bf16[64,4,2,512]{3,2,0,1:T(2,128)(2,1)}), bf16[64,4,2,512]{3,2,0,1:T(2,128)(2,1)S(1)}, u32[]{:S(2)}, u32[]{:S(2)}) async-start(bf16[64,4,2,512]{3,2,0,1:T(2,128)(2,1)} %copy.63), calls=%async_computation.4 | async-start | bytes 1048576 | tf_op jit(solution)/shard_map/all_to_all | solution.py:73
  401.3 219.2 %all-gather.2.cloned.1.call-start = ((), (), s32[]{:S(2)}) async-start(), calls=%async_computation.6 | async-start | bytes 8519680 | tf_op jit(solution)/shard_map/all_gather | solution.py:90
  413.3 117.8 %copy-start.12 = (f32[512]{0:T(512)S(1)}, f32[512]{0:T(512)}, u32[]{:S(2)}) copy-start(f32[512]{0:T(512)} %param.12) | copy-start | bytes 6148
  413.3 119.5 %copy-start.11 = (s32[1,1,64,4,2]{2,4,3,1,0:T(2,128)S(1)}, s32[1,1,64,4,2]{2,4,3,1,0:T(2,128)}, u32[]{:S(2)}) copy-start(s32[1,1,64,4,2]{2,4,3,1,0:T(2,128)} %param.13) | copy-start | bytes 6148
  417.2 128.6 %copy-start.14 = (s32[1,128]{1,0:T(1,128)S(1)}, s32[1,128]{1,0:T(1,128)}, u32[]{:S(2)}) copy-start(s32[1,128]{1,0:T(1,128)} %param.15) | copy-start | bytes 1540
  537.3 28.4 %all-to-all-start = ((bf16[64,4,2,512]{3,2,1,0:T(2,128)(2,1)}), bf16[64,4,2,512]{3,2,1,0:T(2,128)(2,1)S(1)}, u32[]{:S(2)}, u32[]{:S(2)}) async-start(bf16[64,4,2,512]{3,2,1,0:T(2,128)(2,1)} %reshape.908), calls=%async_computation.1 | async-start | bytes 1048576 | tf_op jit(solution)/shard_map/all_to_all | solution.py:41
  566.9 14.2 %all-to-all-start.1 = ((bf16[64,4,2,512]{3,2,0,1:T(2,128)(2,1)}), bf16[64,4,2,512]{3,2,0,1:T(2,128)(2,1)S(1)}, u32[]{:S(2)}, u32[]{:S(2)}) async-start(bf16[64,4,2,512]{3,2,0,1:T(2,128)(2,1)} %copy.60), calls=%async_computation.2 | async-start | bytes 1048576 | tf_op jit(solution)/shard_map/all_to_all | solution.py:40
  571.2 310.8 %all-reduce.6.cloned.1.call-start = ((), (), s32[]{:S(2)}) async-start(), calls=%async_computation.8 | async-start | bytes 4194304
  612.9 7.7 copy-start.4
  620.2 309.0 %all-reduce.4.cloned.1.call-start = ((), (), s32[]{:S(2)}) async-start(), calls=%async_computation.7 | async-start | bytes 262144 | tf_op jit(solution)/shard_map/psum | solution.py:97
  620.6 5.8 copy-start.1
  620.6 7.0 copy-start.3
  627.5 2.3 copy-start.6
  627.5 2.3 copy-start.7
Sparse Core Ops, SparseCore 0:
  339.7 191.3 reduce-scatter.1
  533.9 82.5 all-gather.1
  621.9 260.1 all-reduce.5
  884.2 44.9 all-reduce.3
where the time goes:
time: 938 us; the launch traced here: 937 us
  waiting for transfers between devices  432 us (46%)
  local copies, waits for them, and re-layouts  339 us (36%)
  other arithmetic  62.9 us (7%)
  blocking collectives  38.7 us (4%)
  matrix products  33.1 us (4%)
  starting transfers between devices  17.6 us (2%)
  between operations  14.3 us (2%)
    gather x1, local copies, waits for them, and re-layouts, on_device(): picked_rows = jnp.take(node_major, neighbours.reshape(-1), axis=0)  286 us
    unnamed x5, waiting for transfers between devices  251 us
    reduce_scatter x1, waiting for transfers between devices, on_device(): lax.psum_scatter(contract_rows(feat_rows, w_one[0]) + contract_rows(agg_r...  114 us
    gather x25, local copies, waits for them, and re-layouts, on_device(): picked = flat_table[slot_index[index]].astype(jnp.float32)  34.2 us
    psum x1, waiting for transfers between devices, on_device(): lax.psum(jnp.stack([grad_self, grad_near], axis=0).astype(jnp.bfloat16),...  30.6 us
    all_to_all x1, blocking collectives, on_device(): lax.all_to_all(d_table.reshape(received.shape).astype(jnp.bfloat16), 'fea...  28.5 us
    dot_general x4, matrix products, contract_rows(): lax.dot_general(left, right, (((0,), (0,)), ((), ())), preferred_element_...  24 us
    scatter-add x1, other arithmetic, on_device(): jax.ops.segment_sum(per_slot, slot_index.reshape(-1), num_segments=flat_t...  22.5 us
  transfers between devices with their start and end apart: 7, of which 6 were waited for; matrix products, arithmetic and copies ran while one was open for 10% of the time, Pallas kernels for 0%

commit v1 on v0

v1 whole, which is shorter than its diff:
```python
import jax
import jax.numpy as jnp
from jax import lax
from jax.experimental import pallas as pl
from jax.experimental.pallas import tpu as pltpu
from jax.sharding import Mesh, PartitionSpec as P

BF = jnp.bfloat16
F32 = jnp.float32
NX, NZ, NC, NY = 4, 8, 2, 4
CHIPS = NX * NZ
STEPS = 4
MEAN_STEPS = 8
FIRST_MEANS = 3
FEAT = ("x", "z", "core")
CHIP = ("x", "z")
ALL = ("x", "z", "core", "grp")
LIMIT = 60 << 20


def vmem():
    return pl.BlockSpec()


def unread():
    return pl.BlockSpec(memory_space=pl.ANY)


def smem():
    return pl.BlockSpec(memory_space=pltpu.SMEM)


def call(body, outs, ins, args, name, scratch=(), us=1.0, grid=None, out_specs=None, alias=None):
    extra = {} if grid is None else {"grid": grid}
    if alias:
        extra["input_output_aliases"] = alias
    return pl.pallas_call(
        body,
        out_shape=outs,
        in_specs=ins,
        out_specs=jax.tree.map(lambda _: vmem(), outs) if out_specs is None else out_specs,
        scratch_shapes=list(scratch),
        cost_estimate=pl.CostEstimate(flops=0, bytes_accessed=int(us * 3.6e6), transcendentals=0),
        compiler_params=pltpu.CompilerParams(vmem_limit_bytes=LIMIT),
        name=name,
        **extra,
    )(*args)


def whole(dims):
    return pl.BlockSpec(dims, lambda i: (0,) * len(dims))


def shape(dims, kind):
    return jax.ShapeDtypeStruct(dims, kind)


def shift(value, axis, size, by):
    return lax.ppermute(value, axis, [(s, (s + by) % size) for s in range(size)])


def dot(a, b, ca, cb):
    return lax.dot_general(a, b, (((ca,), (cb,)), ((), ())), preferred_element_type=F32)


def table_kernel(owned, meta, own, sib, tbl):
    core = meta[0]
    first = core == 0
    def step(chip, carry):
        for c in range(NC):
            cols = pl.ds(pl.multiple_of((chip * NC + c) * owned, owned), owned)
            a, b = own[:, cols].astype(F32), sib[:, cols].astype(F32)
            pair = jnp.concatenate([jnp.where(first, a, b), jnp.where(first, b, a)], axis=0)
            tbl[cols, :] = pair.T
        return carry

    lax.fori_loop(0, CHIPS, step, 0, unroll=2)


def own_rows(core, tbl, mine):
    owned = mine.shape[1]

    def copy(chip, carry):
        at = pl.multiple_of((chip * NC + core) * owned, owned)
        mine[chip] = tbl[pl.ds(at, owned), :].astype(BF)
        return carry

    lax.fori_loop(0, CHIPS, copy, 0)


def mean_rows(fanout, first, idx, tbl, out, acc):
    owned = acc.shape[0]
    per = out.shape[0]

    def chunk(c, carry):
        base = ((first + pl.program_id(0)) * per + c) * (fanout * owned)

        def step(b, inner):
            for j in range(16):
                r = b * 16 + j
                rows = [tbl[pl.ds(idx[base + k * owned + r], 1), :] for k in range(fanout)]
                while len(rows) > 1:
                    rows = [
                        rows[i] + rows[i + 1] if i + 1 < len(rows) else rows[i]
                        for i in range(0, len(rows), 2)
                    ]
                acc[pl.ds(r, 1), :] = rows[0]
            return inner

        lax.fori_loop(0, owned // 16, step, 0)
        out[c] = (acc[...] / float(fanout)).astype(BF)
        return carry

    lax.fori_loop(0, per, chunk, 0)


def first_mean_kernel(fanout, meta, idx, tbl, after, out, mine, acc):
    @pl.when(pl.program_id(0) == 0)
    def _():
        own_rows(meta[0], tbl, mine)

    mean_rows(fanout, 0, idx, tbl, out, acc)


def last_mean_kernel(fanout, idx, tbl, begun, after, out, acc):
    mean_rows(fanout, FIRST_MEANS, idx, tbl, out, acc)


def by_row(deg_row, width):
    n = deg_row.shape[1]
    square = jnp.broadcast_to(deg_row[...].astype(F32), (n, n)).T
    return jnp.concatenate([square] * (width // n), axis=1)


def add_product(left, w, acc):
    per = left.shape[0]
    feats = w.shape[2]
    rows = w[...].reshape(per * NC * feats, w.shape[3])
    lhs = jnp.concatenate([left[i] for i in range(per)], axis=1)
    term = dot(lhs, rows, 1, 0)

    @pl.when(pl.program_id(0) == 0)
    def _():
        acc[...] = term

    @pl.when(pl.program_id(0) > 0)
    def _():
        acc[...] += term


def self_kernel(left, w, out):
    add_product(left, w, out)


def node_kernel(
    left, w, self_part, bias, d_self, returned, send, h_out, dpre_out, outgoing, acc
):
    add_product(left, w, acc)

    @pl.when(pl.program_id(0) == STEPS - 1)
    def _():
        pre = self_part[...] + acc[...] + bias[...]
        h = jnp.maximum(pre, 0.0).astype(BF)
        h_out[...] = h
        rows = lax.broadcasted_iota(jnp.int32, (pre.shape[0], send.shape[1]), 0)
        pick = (rows == send[...]).astype(F32).astype(BF)
        d_near = dot(pick, returned[...], 1, 0)
        dpre_out[...] = jnp.where(pre > 0.0, d_self[...] + d_near, 0.0).astype(BF)
        outgoing[...] = dot(pick, h, 0, 0).astype(BF)


def table_grad_kernel(cot, w_two, slot, deg_row, d_table, d_self, counts):
    width = cot.shape[1]
    k_two = slot.shape[1]
    live = lax.broadcasted_iota(jnp.int32, slot.shape[1:], 0) < deg_row[...]
    used = jnp.where(live, slot[0], -1)
    q = lax.broadcasted_iota(jnp.int32, counts.shape, 0)
    total = jnp.zeros(counts.shape, F32)
    for k in range(k_two):
        total = total + (q == used[k : k + 1, :]).astype(F32)
    ct = total.astype(BF)
    counts[...] = ct
    d_self[...] = dot(cot[...], w_two[:width, :], 1, 1)
    scaled = dot(cot[...], w_two[width:, :], 1, 1) / by_row(deg_row, width)
    hi = scaled.astype(BF)
    lo = (scaled - hi.astype(F32)).astype(BF)
    d_table[...] = (dot(ct, hi, 1, 0) + dot(ct, lo, 1, 0)).astype(BF)


def layer_two_kernel(meta, table, counts, deg_row, h, cot, w_two, emb, own, sib):
    width = cot.shape[1]
    agg = (dot(counts[...], table[...], 0, 0) / by_row(deg_row, width)).astype(BF)
    hv = h[...]
    emb[...] = (
        dot(hv, w_two[:width, :], 1, 0) + dot(agg, w_two[width:, :], 1, 0)
    ).astype(BF)
    first = meta[0] == 0
    half = own.shape[0] // 2
    for part, left in enumerate((hv, agg)):
        grad = dot(left, cot[...], 0, 0)
        grad = grad.reshape(half, 2, own.shape[1], width)
        rows = pl.ds(part * half, half)
        own[rows] = jnp.where(first, grad[:, 0], grad[:, 1])
        sib[rows] = jnp.where(first, grad[:, 1], grad[:, 0]).astype(BF)


def weight_grad_kernel(meta, left, d_pre, own, sib):
    lanes = left.shape[2]
    nodes = left.shape[1] // 2
    half = lanes // 2
    first = meta[0] == 0
    d_all = d_pre[...]
    for part in range(2):
        grad = dot(left[0, pl.ds(part * nodes, nodes), :], d_all, 0, 0)
        rows = pl.ds(part * half, half)
        own[0, rows, :] = jnp.where(first, grad[:half], grad[half:])
        sib[0, rows, :] = jnp.where(first, grad[half:], grad[:half])
    bias = jnp.sum(d_all.astype(F32), axis=0, keepdims=True)
    tail = jnp.broadcast_to(bias, (16, bias.shape[1]))
    own[0, pl.ds(lanes, 16), :] = tail
    sib[0, pl.ds(lanes, 16), :] = tail


def core_sum_kernel(one_own, one_recv, two_own, two_recv, out):
    rows = one_own.shape[1]
    out[:, :rows, :] = (one_own[...] + one_recv[...]).astype(BF)
    out[:, rows:, :] = (two_own[...] + two_recv[...].astype(F32)).astype(BF)


def sum_first(ref):
    total = ref[0].astype(F32)
    for i in range(1, ref.shape[0]):
        total = total + ref[i].astype(F32)
    return total


def x_sum_kernel(parts, out):
    total = sum_first(parts).astype(BF)
    n = parts.shape[1] - out.shape[1]
    two = n * NY // (NY - 1)
    one = parts.shape[1] - two
    each = two // NY
    per = each // NZ
    to = lax.broadcasted_iota(jnp.int32, (two, two), 0)
    at = lax.broadcasted_iota(jnp.int32, (two, two), 1)
    source = (lax.rem(lax.div(to, per), NZ) * NY + lax.div(to, each)) * per + lax.rem(to, per)
    order = (at == source).astype(F32).astype(BF)
    moved = dot(order, total[one:], 1, 0).astype(BF)
    for y in range(NY):
        out[y, :one, :] = total[:one]
        out[y, one:, :] = moved[y * each : (y + 1) * each]


def y_sum_kernel(parts, grad, bias, two):
    total = sum_first(parts)
    half = grad.shape[1]
    grad[0] = total[:half]
    grad[1] = total[half : 2 * half]
    bias[...] = total[2 * half : 2 * half + 1]
    two[...] = total[2 * half + 16 :]


def all_to_all(value, axes):
    return lax.all_to_all(value, axes, split_axis=0, concat_axis=0, tiled=True)


def on_device(features, nbr_one, w_one, b_one, send_rows, nbr_slot, degree, w_two, cotangent):
    local = features[0]
    feats, group_nodes = local.shape
    fanout = nbr_one.shape[1]
    width = w_two.shape[1]
    owned = cotangent.shape[1]
    lanes = NC * feats
    per = CHIPS // STEPS
    core = lax.axis_index("core")
    meta = jnp.full((1,), core, jnp.int32)
    swap = lambda v: shift(v, "core", NC, 1)

    sibling = swap(local)
    w_all = lax.all_gather(w_one.reshape(-1, width), FEAT, axis=0, tiled=True)
    w_all = w_all.reshape(CHIPS * NC, 2, feats, width)

    deg_row = degree[0][None, :]
    cot = cotangent[0]
    slots = CHIPS * NC * NY * send_rows.shape[-1]
    d_table, d_self, counts = call(
        table_grad_kernel,
        (shape((slots, width), BF), shape((owned, width), F32), shape((slots, owned), BF)),
        [vmem()] * 4,
        (cot, w_two, nbr_slot, deg_row),
        "table_grad", us=3.0,
    )

    def exchange(rows):
        return all_to_all(rows.reshape(CHIPS * NC * NY, -1, width), ALL).reshape(-1, width)

    returned = exchange(d_table)

    tbl = call(
        lambda *refs: table_kernel(owned, *refs),
        shape((group_nodes, lanes), F32),
        [smem(), vmem(), vmem()],
        (meta, local, sibling),
        "node_table", us=6.0,
    )
    by_device = nbr_one[0].reshape(fanout, CHIPS, NC, owned)
    idx = lax.dynamic_index_in_dim(by_device, core, 2, keepdims=False)
    idx = idx.transpose(1, 0, 2).reshape(-1)
    mean_shape = shape((CHIPS, owned, lanes), BF)
    mean_per = CHIPS // MEAN_STEPS
    acc = [pltpu.VMEM((owned, lanes), F32)]
    us_per = idx.shape[0] * 1e-3 / MEAN_STEPS
    begun, mine = call(
        lambda *refs: first_mean_kernel(fanout, *refs),
        (mean_shape, mean_shape),
        [smem(), smem(), whole(tbl.shape), unread()],
        (meta, idx, tbl, d_table),
        "mean_first", acc, us_per * FIRST_MEANS, (FIRST_MEANS,),
        (pl.BlockSpec((mean_per, owned, lanes), lambda i: (i, 0, 0)), whole(mean_shape.shape)),
    )
    feats_here = all_to_all(mine, CHIP)
    last = MEAN_STEPS - FIRST_MEANS
    means = call(
        lambda *refs: last_mean_kernel(fanout, *refs),
        mean_shape,
        [smem(), whole(tbl.shape), unread(), unread()],
        (idx, tbl, begun, returned),
        "mean_last", acc, us_per * last, (last,),
        pl.BlockSpec((mean_per, owned, lanes), lambda i: (i + FIRST_MEANS, 0, 0)),
        {2: 0},
    )
    means_here = all_to_all(means, CHIP)

    left_spec = pl.BlockSpec((per, owned, lanes), lambda i: (i, 0, 0))

    def w_spec(part):
        return pl.BlockSpec((per * NC, 1, feats, width), lambda i: (i, part, 0, 0))

    self_part = call(
        self_kernel, shape((owned, width), F32), [left_spec, w_spec(0)], (feats_here, w_all),
        "self_part", us=4.0, grid=(STEPS,), out_specs=whole((owned, width)),
    )
    send = send_rows[0, 0].reshape(1, -1)
    bias_row = b_one[None, :]
    ins = (self_part, bias_row, d_self, returned, send)
    outs = (shape((owned, width), BF), shape((owned, width), BF), shape((slots, width), BF))
    h_one, d_pre, outgoing = call(
        node_kernel,
        outs,
        [left_spec, w_spec(1)] + [whole(v.shape) for v in ins],
        (means_here, w_all, *ins),
        "node_update",
        [pltpu.VMEM((owned, width), F32)],
        us=4.0, grid=(STEPS,), out_specs=tuple(whole(o.shape) for o in outs),
    )
    d_pre_z = lax.all_gather(d_pre, "z", axis=0, tiled=True)
    both = jnp.concatenate(
        [mine.reshape(NX, NZ * owned, lanes), means.reshape(NX, NZ * owned, lanes)], axis=1
    )
    both, table = lax.optimization_barrier((both, exchange(outgoing)))
    left = all_to_all(both, "x")

    block_rows = 2 * width // (CHIPS * NC)
    emb, two_own, two_sib = call(
        layer_two_kernel,
        (
            shape((owned, width), BF),
            shape((CHIPS, block_rows, width), F32),
            shape((CHIPS, block_rows, width), BF),
        ),
        [smem()] + [vmem()] * 6,
        (meta, table, counts, deg_row, h_one, cot, w_two),
        "layer_two", us=3.0,
    )
    d_pre_z, two_sib = lax.optimization_barrier((d_pre_z, two_sib))
    two_recv = swap(two_sib)

    rows = 2 * feats + 16
    one_spec = pl.BlockSpec((1, rows, width), lambda i: (i, 0, 0))
    one_own, one_sib = call(
        weight_grad_kernel,
        (shape((NX, rows, width), F32), shape((NX, rows, width), F32)),
        [
            smem(), pl.BlockSpec((1, 2 * NZ * owned, lanes), lambda i: (i, 0, 0)),
            whole(d_pre_z.shape),
        ],
        (meta, left, d_pre_z),
        "weight_grad",
        us=4.0, grid=(NX,), out_specs=(one_spec, one_spec),
    )
    one_recv = swap(one_sib)
    two_rows = NZ * block_rows
    sums = call(
        core_sum_kernel,
        shape((NX, rows + two_rows, width), BF),
        [vmem()] * 4,
        (
            one_own, one_recv, two_own.reshape(NX, two_rows, width),
            two_recv.reshape(NX, two_rows, width),
        ),
        "core_sum",
    )
    sums = call(
        x_sum_kernel, shape((NY, rows + two_rows // NY, width), BF), [vmem()],
        (all_to_all(sums, "x"),), "x_sum",
    )
    grad_w_one, grad_b_one, two = call(
        y_sum_kernel,
        (
            shape((2, feats, width), F32), shape((1, width), F32),
            shape((two_rows // NY, width), F32),
        ),
        [vmem()],
        (all_to_all(sums, "grp"),),
        "y_sum",
    )
    grad_w_two = jnp.sum(all_to_all(two.reshape(NZ, -1, width), "z"), axis=0)
    return emb[None], grad_w_one, grad_b_one[0], grad_w_two


def solution(mesh):
    parts = Mesh(mesh.devices.reshape(NX, NZ, NC, NY), ALL)
    return jax.shard_map(
        on_device,
        mesh=parts,
        in_specs=(
            P("grp", FEAT, None),
            P("grp", None, None),
            P(None, FEAT, None),
            P(),
            P("grp", FEAT, None, None, None),
            P("grp", None, FEAT),
            P("grp", FEAT),
            P(),
            P("grp", FEAT, None),
        ),
        out_specs=(P("grp", FEAT, None), P(None, FEAT, None), P(), P(ALL, None)),
        check_vma=False,
    )
```

time: 938 us -> 283 us (0.30)
  waiting for transfers between devices: 432 us -> 72 us
  local copies, waits for them, and re-layouts: 339 us -> 14.7 us
  Pallas kernels: 0 us -> 81.4 us
  other arithmetic: 62.9 us -> 2.11 us
  starting transfers between devices: 17.6 us -> 51.1 us
  matrix products: 33.1 us -> 0 us
    gather x28 -> x0, local copies, waits for them, and re-layouts: 323 us -> none  [the longest x1 286 us: on_device(): picked_rows = jnp.take(node_major, neighbours.reshape(-1), axis=0)]
    unnamed x5 -> x2, waiting for transfers between devices: 251 us -> 1.38 us
    reduce_scatter x1 -> x0, waiting for transfers between devices: 114 us -> none  [on_device(): lax.psum_scatter(contract_rows(feat_rows, w_one[0]) + contract_rows(agg_r...]
    pallas_call x0 -> x11, Pallas kernels: none -> 81.4 us  [call(): pl.pallas_call(body, out_shape=outs, in_specs=ins, out_specs=jax.tree.map...]
    all_to_all x3 -> x5, starting transfers between devices: 17.2 us -> 50.4 us  [all_to_all(): return lax.all_to_all(value, axes, split_axis=0, concat_axis=0, tiled=True)]
    dot_general x10 -> x0, matrix products: 33.1 us -> none  [the longest x4 24 us: contract_rows(): lax.dot_general(left, right, (((0,), (0,)), ((), ())), preferred_element_...]
    psum x1 -> x0, waiting for transfers between devices: 30.6 us -> none  [on_device(): lax.psum(jnp.stack([grad_self, grad_near], axis=0).astype(jnp.bfloat16),...]
    scatter-add x2 -> x0, other arithmetic: 26.3 us -> none  [the longest x1 22.5 us: on_device(): jax.ops.segment_sum(per_slot, slot_index.reshape(-1), num_segments=flat_t...]
  transfers between devices with their start and end apart: 7 -> 10, of which waited for: 6 -> 8; matrix products, arithmetic and copies ran while one was open for 10% -> 3% of each run, Pallas kernels for 0% -> 22%
where the time goes in v1:
time: 283 us; the launch traced here: 282 us
  Pallas kernels  81.4 us (29%)
  waiting for transfers between devices  72 us (25%)
  starting transfers between devices  51.1 us (18%)
  blocking collectives  46.7 us (17%)
  local copies, waits for them, and re-layouts  14.7 us (5%)
  between operations  14.2 us (5%)
    pallas_call x11, Pallas kernels, call(): pl.pallas_call(body, out_shape=outs, in_specs=ins, out_specs=jax.tree.map...  81.4 us
    all_to_all x5, waiting for transfers between devices, all_to_all(): return lax.all_to_all(value, axes, split_axis=0, concat_axis=0, tiled=True)  52.5 us
    all_to_all x5, starting transfers between devices, all_to_all(): return lax.all_to_all(value, axes, split_axis=0, concat_axis=0, tiled=True)  50.4 us
    all_to_all x3, blocking collectives, all_to_all(): return lax.all_to_all(value, axes, split_axis=0, concat_axis=0, tiled=True)  46.7 us
    all_gather x1, waiting for transfers between devices, on_device(): d_pre_z = lax.all_gather(d_pre, 'z', axis=0, tiled=True)  13.2 us
    unnamed x24, local copies, waits for them, and re-layouts  5.88 us
  transfers between devices with their start and end apart: 10, of which 8 were waited for; matrix products, arithmetic and copies ran while one was open for 3% of the time, Pallas kernels for 22%

profile of v1, /device:TPU:2, one launch (start us, length us, event | category | flops | bytes accessed | tf_op | source)
XLA Modules:
  0.0 282.2 jit_solution(2161030375847984248)
XLA Ops:
  9.3 3.4 %table_grad.1 = (bf16[512,512]{1,0:T(8,128)(2,1)}, f32[128,512]{1,0:T(8,128)}, bf16[512,128]{1,0:T(8,128)(2,1)}) custom-call(bf16[128,512]{1,0:T(8,128)(2,1)} %bitcast.28, bf16[1024,512]{1,0:T(8,128)(2,1)} %w_two.3, s32[1,25,128]{2,1,0:T(8,128)} %copy.17.slot, s32[1,128]{1,0:T(1,128)} %deg_row.3), custom_call_target="tpu_custom_call" | custom-call | bytes 10800000 | tf_op jit(solution)/shard_map/table_grad/pallas_call | solution.py:37
  14.8 14.8 %all-to-all-start = ((bf16[256,2,512]{2,1,0:T(2,128)(2,1)}), bf16[256,2,512]{2,1,0:T(2,128)(2,1)S(1)}, u32[]{:S(2)}, u32[]{:S(2)}) async-start(bf16[256,2,512]{2,1,0:T(2,128)(2,1)} %reshape.46), calls=%async_computation | async-start | bytes 1048576 | tf_op jit(solution)/shard_map/all_to_all | solution.py:264
  31.5 5.6 %node_table.1.refs_2_.refs_1_ = f32[8192,128]{1,0:T(8,128)} custom-call(s32[1]{0:T(128)} %bitcast.refs_0_.meta, bf16[64,8192]{1,0:T(8,128)(2,1)} %bitcast.24, bf16[64,8192]{1,0:T(8,128)(2,1)} %copy-done.7), custom_call_target="tpu_custom_call" | custom-call | bytes 21600000 | tf_op jit(solution)/shard_map/node_table/pallas_call | solution.py:37
  37.1 18.8 %mean_first.1 = (bf16[32,128,128]{2,1,0:T(8,128)(2,1)}, bf16[32,128,128]{2,1,0:T(8,128)(2,1)}) custom-call(s32[1]{0:T(128)} %bitcast.refs_0_.meta, s32[40960]{0:T(1024)} %reshape.44.refs_1_.refs_0_, f32[8192,128]{1,0:T(8,128)} %node_table.1.refs_2_.refs_1_, bf16[512,512]{1,0:T(8,128)(2,1)} %get-tuple-element.24.refs_3_), custom_call_target="tpu_custom_call" | custom-call | bytes 55296000 | tf_op jit(solution)/shard_map/mean_first/pallas_call | solution.py:37
  55.9 10.7 %all-to-all-start.2 = ((bf16[32,128,128]{2,1,0:T(8,128)(2,1)}), bf16[32,128,128]{2,1,0:T(8,128)(2,1)S(1)}, u32[]{:S(2)}, u32[]{:S(2)}) async-start(bf16[32,128,128]{2,1,0:T(8,128)(2,1)} %get-tuple-element.25), calls=%async_computation.2 | async-start | bytes 2097152 | tf_op jit(solution)/shard_map/all_to_all | solution.py:264
  67.6 27.6 %mean_last.1 = bf16[32,128,128]{2,1,0:T(8,128)(2,1)} custom-call(s32[40960]{0:T(1024)} %reshape.44.refs_1_.refs_0_, f32[8192,128]{1,0:T(8,128)} %node_table.1.refs_2_.refs_1_, bf16[32,128,128]{2,1,0:T(8,128)(2,1)} %get-tuple-element.26.refs_2_, bf16[512,512]{1,0:T(8,128)(2,1)} %reshape.47.refs_3_.returned), custom_call_target="tpu_custom_call", output_to_operand_aliasing={{}: (2, {})} | custom-call | bytes 92160000 | tf_op jit(solution)/shard_map/mean_last/pallas_call | solution.py:37
  95.2 8.1 %all-to-all-done.2.left = bf16[32,128,128]{2,1,0:T(8,128)(2,1)S(1)} async-done(((bf16[32,128,128]{2,1,0:T(8,128)(2,1)}), bf16[32,128,128]{2,1,0:T(8,128)(2,1)S(1)}, u32[]{:S(2)}, u32[]{:S(2)}) %all-to-all-start.2) | async-done | bytes 1048608 | tf_op jit(solution)/shard_map/all_to_all | solution.py:264
  103.3 8.3 %all-to-all-start.1 = ((bf16[32,128,128]{2,1,0:T(8,128)(2,1)}), bf16[32,128,128]{2,1,0:T(8,128)(2,1)S(1)}, u32[]{:S(2)}, u32[]{:S(2)}) async-start(bf16[32,128,128]{2,1,0:T(8,128)(2,1)} %mean_last.1), calls=%async_computation.1 | async-start | bytes 2097152 | tf_op jit(solution)/shard_map/all_to_all | solution.py:264
  114.1 4.5 %self_part.1 = f32[128,512]{1,0:T(8,128)} custom-call(bf16[32,128,128]{2,1,0:T(8,128)(2,1)} %copy-done.3, bf16[64,2,64,512]{3,2,1,0:T(8,128)(2,1)} %bitcast.19), custom_call_target="tpu_custom_call" | custom-call | bytes 14400000 | tf_op jit(solution)/shard_map/self_part/pallas_call | solution.py:37
  118.7 18.9 %all-to-all-done.1.left = bf16[32,128,128]{2,1,0:T(8,128)(2,1)S(1)} async-done(((bf16[32,128,128]{2,1,0:T(8,128)(2,1)}), bf16[32,128,128]{2,1,0:T(8,128)(2,1)S(1)}, u32[]{:S(2)}, u32[]{:S(2)}) %all-to-all-start.1) | async-done | bytes 1048608 | tf_op jit(solution)/shard_map/all_to_all | solution.py:264
  138.6 5.4 %node_update.1 = (bf16[128,512]{1,0:T(8,128)(2,1)}, bf16[128,512]{1,0:T(8,128)(2,1)}, bf16[512,512]{1,0:T(8,128)(2,1)}) custom-call(bf16[32,128,128]{2,1,0:T(8,128)(2,1)} %copy-done.4, bf16[64,2,64,512]{3,2,1,0:T(8,128)(2,1)} %bitcast.20, f32[128,512]{1,0:T(8,128)} %self_part.1, f32[1,512]{1,0:T(1,128)} %bitcast.31, f32[128,512]{1,0:T(8,128)} %get-tuple-element.27.d_self, ...), custom_call_target="tpu_custom_call" | custom-call | bytes 14400000 | tf_op jit(solution)/shard_map/node_update/pallas_call | solution.py:37
  146.3 10.4 %all-to-all-start.3 = ((bf16[256,2,512]{2,1,0:T(2,128)(2,1)}), bf16[256,2,512]{2,1,0:T(2,128)(2,1)S(1)}, u32[]{:S(2)}, u32[]{:S(2)}) async-start(bf16[256,2,512]{2,1,0:T(2,128)(2,1)} %reshape.51), calls=%async_computation.3 | async-start | bytes 1048576 | tf_op jit(solution)/shard_map/all_to_all | solution.py:264
  159.0 17.1 %all-to-all-done.3 = bf16[256,2,512]{2,1,0:T(2,128)(2,1)S(1)} async-done(((bf16[256,2,512]{2,1,0:T(2,128)(2,1)}), bf16[256,2,512]{2,1,0:T(2,128)(2,1)S(1)}, u32[]{:S(2)}, u32[]{:S(2)}) %all-to-all-start.3) | async-done | bytes 524320 | tf_op jit(solution)/shard_map/all_to_all | solution.py:264
  177.0 6.2 %all-to-all-start.4 = ((bf16[4,2048,128]{2,1,0:T(8,128)(2,1)}), bf16[4,2048,128]{2,1,0:T(8,128)(2,1)S(1)}, u32[]{:S(2)}, u32[]{:S(2)}) async-start(bf16[4,2048,128]{2,1,0:T(8,128)(2,1)} %pad_maximum_fusion), calls=%async_computation.4 | async-start | bytes 4194304 | tf_op jit(solution)/shard_map/all_to_all | solution.py:264
  183.2 3.5 %layer_two.1 = (bf16[128,512]{1,0:T(8,128)(2,1)}, f32[32,16,512]{2,1,0:T(8,128)}, bf16[32,16,512]{2,1,0:T(8,128)(2,1)}) custom-call(s32[1]{0:T(128)} %bitcast.refs_0_.meta, bf16[512,512]{1,0:T(8,128)(2,1)} %reshape.52.table, bf16[512,128]{1,0:T(8,128)(2,1)} %get-tuple-element.30.counts, s32[1,128]{1,0:T(1,128)} %deg_row.3, ...), custom_call_target="tpu_custom_call" | custom-call | bytes 10800000 | tf_op jit(solution)/shard_map/layer_two/pallas_call | solution.py:37
  186.7 13.2 %all-gather.5.cloned.1.call-done.d_pre = bf16[1024,512]{1,0:T(8,128)(2,1)} async-done(((bf16[128,512]{1,0:T(8,128)(2,1)}), bf16[1024,512]{1,0:T(8,128)(2,1)}) %all-gather.5.cloned.1.call-update) | async-done | bytes 1048592 | tf_op jit(solution)/shard_map/all_gather | solution.py:356
  199.9 8.5 %all-to-all-done.4.left = bf16[4,2048,128]{2,1,0:T(8,128)(2,1)S(1)} async-done(((bf16[4,2048,128]{2,1,0:T(8,128)(2,1)}), bf16[4,2048,128]{2,1,0:T(8,128)(2,1)S(1)}, u32[]{:S(2)}, u32[]{:S(2)}) %all-to-all-start.4) | async-done | bytes 2097184 | tf_op jit(solution)/shard_map/all_to_all | solution.py:264
  209.7 5.1 %weight_grad.1 = (f32[4,144,512]{2,1,0:T(8,128)}, f32[4,144,512]{2,1,0:T(8,128)}) custom-call(s32[1]{0:T(128)} %bitcast.refs_0_.meta, bf16[4,2048,128]{2,1,0:T(8,128)(2,1)} %copy-done.2, bf16[1024,512]{1,0:T(8,128)(2,1)} %all-gather.5.cloned.1.call-done.d_pre), custom_call_target="tpu_custom_call" | custom-call | bytes 14400000 | tf_op jit(solution)/shard_map/weight_grad/pallas_call | solution.py:37
  215.3 3.1 %collective-permute-done.2 = bf16[32,16,512]{2,1,0:T(8,128)(2,1)S(1)} collective-permute-done((bf16[32,16,512]{2,1,0:T(8,128)(2,1)S(1)}, bf16[32,16,512]{2,1,0:T(8,128)(2,1)S(1)}, u32[]{:S(2)}, u32[]{:S(2)}) %collective-permute-start.2) | collective-permute-done | bytes 524320 | tf_op jit(solution)/shard_map/ppermute | solution.py:59
  219.6 3.3 %core_sum.1 = bf16[4,272,512]{2,1,0:T(8,128)(2,1)} custom-call(f32[4,144,512]{2,1,0:T(8,128)} %get-tuple-element.37.one_own, f32[4,144,512]{2,1,0:T(8,128)} %copy-done.6, f32[4,128,512]{2,1,0:T(8,128)} %bitcast.25, bf16[4,128,512]{2,1,0:T(8,128)(2,1)} %bitcast.27), custom_call_target="tpu_custom_call" | custom-call | bytes 3600000 | tf_op jit(solution)/shard_map/core_sum/pallas_call | solution.py:37
  222.9 20.7 %all_to_all.40.parts = bf16[4,272,512]{2,1,0:T(8,128)(2,1)} all-to-all(bf16[4,272,512]{2,1,0:T(8,128)(2,1)} %core_sum.1), channel_id=1, replica_groups=mesh['x'=4,'z'=8,'core'=2,'grp'=4] {'x'}, dimensions={0} | all-to-all | bytes 2228224 | tf_op jit(solution)/shard_map/all_to_all | solution.py:264
  243.6 2.4 x_sum.1
  246.0 15.3 %all_to_all.41.parts = bf16[4,176,512]{2,1,0:T(8,128)(2,1)} all-to-all(bf16[4,176,512]{2,1,0:T(8,128)(2,1)} %x_sum.1), channel_id=1, replica_groups=mesh['x'=4,'z'=8,'core'=2,'grp'=4] {'grp'}, dimensions={0} | all-to-all | bytes 1441792 | tf_op jit(solution)/shard_map/all_to_all | solution.py:264
  264.0 10.8 %all_to_all.42 = f32[8,4,512]{2,1,0:T(4,128)S(1)} all-to-all(f32[8,4,512]{2,1,0:T(4,128)S(1)} %reshape.55), channel_id=1, replica_groups=mesh['x'=4,'z'=8,'core'=2,'grp'=4] {'z'}, dimensions={0} | all-to-all | bytes 131072 | tf_op jit(solution)/shard_map/all_to_all | solution.py:264
  (47 shorter events, 22.6 us)
Async XLA Ops:
  7.2 22.4 %copy-start = (s32[1,10,8192]{2,0,1:T(1,128)S(1)}, s32[1,10,8192]{2,0,1:T(1,128)}, u32[]{:S(2)}) copy-start(s32[1,10,8192]{2,0,1:T(1,128)} %param.10) | copy-start | bytes 983044
  7.2 107.0 %all-gather.3.cloned.1.call-start = ((), (), s32[]{:S(2)}) async-start(), calls=%async_computation.8 | async-start | bytes 8519680 | tf_op jit(solution)/shard_map/all_gather | solution.py:280
  7.9 22.6 %collective-permute-start = (bf16[64,8192]{1,0:T(8,128)(2,1)}, bf16[64,8192]{1,0:T(8,128)(2,1)S(1)}, u32[]{:S(2)}, u32[]{:S(2)}) collective-permute-start(bf16[64,8192]{1,0:T(8,128)(2,1)} %bitcast.23), channel_id=1, source_target_pairs={{0,4},{4,0},{1,5},{5,1},{2,6},{6,2},{3,7},{7,3},{8,12},{12,8},{9,1... | collective-permute-start | bytes 3145736 | tf_op jit(solution)/shard_map/ppermute | solution.py:59
  14.8 41.1 %all-to-all-start = ((bf16[256,2,512]{2,1,0:T(2,128)(2,1)}), bf16[256,2,512]{2,1,0:T(2,128)(2,1)S(1)}, u32[]{:S(2)}, u32[]{:S(2)}) async-start(bf16[256,2,512]{2,1,0:T(2,128)(2,1)} %reshape.46), calls=%async_computation | async-start | bytes 1048576 | tf_op jit(solution)/shard_map/all_to_all | solution.py:264
  30.5 1.0 copy-start.7
  55.9 47.4 %all-to-all-start.2 = ((bf16[32,128,128]{2,1,0:T(8,128)(2,1)}), bf16[32,128,128]{2,1,0:T(8,128)(2,1)S(1)}, u32[]{:S(2)}, u32[]{:S(2)}) async-start(bf16[32,128,128]{2,1,0:T(8,128)(2,1)} %get-tuple-element.25), calls=%async_computation.2 | async-start | bytes 2097152 | tf_op jit(solution)/shard_map/all_to_all | solution.py:264
  95.2 16.4 %copy-start.9 = (s32[1,1,64,4,2]{2,4,3,1,0:T(2,128)S(1)}, s32[1,1,64,4,2]{2,4,3,1,0:T(2,128)}, u32[]{:S(2)}) copy-start(s32[1,1,64,4,2]{2,4,3,1,0:T(2,128)} %param.13) | copy-start | bytes 6148
  103.3 10.9 %copy-start.3 = (bf16[32,128,128]{2,1,0:T(8,128)(2,1)}, bf16[32,128,128]{2,1,0:T(8,128)(2,1)S(1)}, u32[]{:S(2)}) copy-start(bf16[32,128,128]{2,1,0:T(8,128)(2,1)S(1)} %all-to-all-done.2.left) | copy-start | bytes 3145732
  103.3 34.3 %all-to-all-start.1 = ((bf16[32,128,128]{2,1,0:T(8,128)(2,1)}), bf16[32,128,128]{2,1,0:T(8,128)(2,1)S(1)}, u32[]{:S(2)}, u32[]{:S(2)}) async-start(bf16[32,128,128]{2,1,0:T(8,128)(2,1)} %mean_last.1), calls=%async_computation.1 | async-start | bytes 2097152 | tf_op jit(solution)/shard_map/all_to_all | solution.py:264
  137.6 1.0 copy-start.4
  144.1 13.4 %copy-start.1 = (bf16[32,128,128]{2,1,0:T(8,128)(2,1)S(1)}, bf16[32,128,128]{2,1,0:T(8,128)(2,1)}, u32[]{:S(2)}) copy-start(bf16[32,128,128]{2,1,0:T(8,128)(2,1)} %mean_last.1) | copy-start | bytes 3145732
  144.1 13.4 %copy-start.5 = (bf16[32,128,128]{2,1,0:T(8,128)(2,1)S(1)}, bf16[32,128,128]{2,1,0:T(8,128)(2,1)}, u32[]{:S(2)}) copy-start(bf16[32,128,128]{2,1,0:T(8,128)(2,1)} %get-tuple-element.25) | copy-start | bytes 3145732
  146.3 29.8 %all-to-all-start.3 = ((bf16[256,2,512]{2,1,0:T(2,128)(2,1)}), bf16[256,2,512]{2,1,0:T(2,128)(2,1)S(1)}, u32[]{:S(2)}, u32[]{:S(2)}) async-start(bf16[256,2,512]{2,1,0:T(2,128)(2,1)} %reshape.51), calls=%async_computation.3 | async-start | bytes 1048576 | tf_op jit(solution)/shard_map/all_to_all | solution.py:264
  156.7 43.2 %all-gather.5.cloned.1.call-start = ((), (), s32[]{:S(2)}) async-start(), calls=%async_computation.9 | async-start | bytes 1179648 | tf_op jit(solution)/shard_map/all_gather | solution.py:356
  177.0 31.3 %all-to-all-start.4 = ((bf16[4,2048,128]{2,1,0:T(8,128)(2,1)}), bf16[4,2048,128]{2,1,0:T(8,128)(2,1)S(1)}, u32[]{:S(2)}, u32[]{:S(2)}) async-start(bf16[4,2048,128]{2,1,0:T(8,128)(2,1)} %pad_maximum_fusion), calls=%async_computation.4 | async-start | bytes 4194304 | tf_op jit(solution)/shard_map/all_to_all | solution.py:264
  186.7 28.1 %copy-start.10 = (bf16[32,16,512]{2,1,0:T(8,128)(2,1)S(1)}, bf16[32,16,512]{2,1,0:T(8,128)(2,1)}, u32[]{:S(2)}) copy-start(bf16[32,16,512]{2,1,0:T(8,128)(2,1)} %get-tuple-element.40) | copy-start | bytes 1572868
  208.3 1.4 copy-start.2
  214.8 3.8 %collective-permute-start.1 = (f32[4,144,512]{2,1,0:T(8,128)}, f32[4,144,512]{2,1,0:T(8,128)S(1)}, u32[]{:S(2)}, u32[]{:S(2)}) collective-permute-start(f32[4,144,512]{2,1,0:T(8,128)} %get-tuple-element.38), channel_id=1, source_target_pairs={{0,4},{4,0},{1,5},{5,1},{2,6},{6,2},{3,7},{7,3},{8,12},{12,8},{9,1... | collective-permute-start | bytes 3538952 | tf_op jit(solution)/shard_map/ppermute | solution.py:59
  214.8 3.6 %collective-permute-start.2 = (bf16[32,16,512]{2,1,0:T(8,128)(2,1)S(1)}, bf16[32,16,512]{2,1,0:T(8,128)(2,1)S(1)}, u32[]{:S(2)}, u32[]{:S(2)}) collective-permute-start(bf16[32,16,512]{2,1,0:T(8,128)(2,1)S(1)} %copy-done.10), channel_id=1, source_target_pairs={{0,4},{4,0},{1,5},{5,1},{2,6},{6,2},{3,7},{7,3},{8,12},{12,8},{9,1... | collective-permute-start | bytes 1572872 | tf_op jit(solution)/shard_map/ppermute | solution.py:59
  218.4 0.8 copy-start.8
  218.6 1.0 copy-start.6
Sparse Core Ops, SparseCore 0:
  10.8 103.2 all-gather.2
  159.3 40.5 all-gather.4

commit v2 on v1

--- a/solution.py
+++ b/solution.py
@@ -11,7 +11,7 @@
 CHIPS = NX * NZ
 STEPS = 4
 MEAN_STEPS = 8
-FIRST_MEANS = 3
+FIRST_MEANS = 2
 FEAT = ("x", "z", "core")
 CHIP = ("x", "z")
 ALL = ("x", "z", "core", "grp")
@@ -204,60 +204,67 @@
         sib[rows] = jnp.where(first, grad[:, 1], grad[:, 0]).astype(BF)
 
 
-def weight_grad_kernel(meta, left, d_pre, own, sib):
-    lanes = left.shape[2]
-    nodes = left.shape[1] // 2
+def two_sum_kernel(own, recv, out):
+    n = own.shape[1]
+    for x in range(NX):
+        for z in range(NZ):
+            total = own[x * NZ + z] + recv[x * NZ + z].astype(F32)
+            out[z, pl.ds(x * n, n), :] = total.astype(BF)
+
+
+def weight_grad_kernel(meta, *refs):
+    feats, means = refs[:NX], refs[NX : 2 * NX]
+    d_pre, own, sib = refs[2 * NX :]
+    lanes = feats[0].shape[2]
     half = lanes // 2
     first = meta[0] == 0
     d_all = d_pre[...]
-    for part in range(2):
-        grad = dot(left[0, pl.ds(part * nodes, nodes), :], d_all, 0, 0)
-        rows = pl.ds(part * half, half)
-        own[0, rows, :] = jnp.where(first, grad[:half], grad[half:])
-        sib[0, rows, :] = jnp.where(first, grad[half:], grad[:half])
     bias = jnp.sum(d_all.astype(F32), axis=0, keepdims=True)
     tail = jnp.broadcast_to(bias, (16, bias.shape[1]))
-    own[0, pl.ds(lanes, 16), :] = tail
-    sib[0, pl.ds(lanes, 16), :] = tail
-
-
-def core_sum_kernel(one_own, one_recv, two_own, two_recv, out):
-    rows = one_own.shape[1]
-    out[:, :rows, :] = (one_own[...] + one_recv[...]).astype(BF)
-    out[:, rows:, :] = (two_own[...] + two_recv[...].astype(F32)).astype(BF)
-
-
-def sum_first(ref):
-    total = ref[0].astype(F32)
-    for i in range(1, ref.shape[0]):
-        total = total + ref[i].astype(F32)
-    return total
-
-
-def x_sum_kernel(parts, out):
-    total = sum_first(parts).astype(BF)
-    n = parts.shape[1] - out.shape[1]
-    two = n * NY // (NY - 1)
-    one = parts.shape[1] - two
-    each = two // NY
-    per = each // NZ
-    to = lax.broadcasted_iota(jnp.int32, (two, two), 0)
-    at = lax.broadcasted_iota(jnp.int32, (two, two), 1)
-    source = (lax.rem(lax.div(to, per), NZ) * NY + lax.div(to, each)) * per + lax.rem(to, per)
-    order = (at == source).astype(F32).astype(BF)
-    moved = dot(order, total[one:], 1, 0).astype(BF)
-    for y in range(NY):
-        out[y, :one, :] = total[:one]
-        out[y, one:, :] = moved[y * each : (y + 1) * each]
-
-
-def y_sum_kernel(parts, grad, bias, two):
-    total = sum_first(parts)
+    for d in range(NX):
+        e = (NX - d) % NX
+        for part, left in enumerate((feats[d], means[d])):
+            grad = dot(left[...].reshape(-1, lanes), d_all, 0, 0)
+            rows = pl.ds(part * half, half)
+            own[e, rows, :] = jnp.where(first, grad[:half], grad[half:])
+            sib[e, rows, :] = jnp.where(first, grad[half:], grad[:half])
+        own[e, pl.ds(lanes, 16), :] = tail
+        sib[e, pl.ds(lanes, 16), :] = tail
+
+
+def core_sum_kernel(meta, own, recv, two, p0, p1, p2, p3):
+    rows = own.shape[1]
+    n = two.shape[1] // NX
+    for e, out in enumerate((p0, p1, p2, p3)):
+        out[:rows, :] = (own[e] + recv[e]).astype(BF)
+        at = pl.multiple_of(lax.rem(meta[1] + e, NX) * n, n)
+        total = two[0, pl.ds(at, n), :].astype(F32)
+        for z in range(1, NZ):
+            total = total + two[z, pl.ds(at, n), :].astype(F32)
+        out[rows:, :] = total.astype(BF)
+
+
+def four_sum(parts):
+    p0, p1, p2, p3 = [p[...].astype(F32) for p in parts]
+    return (p0 + p2) + (p1 + p3)
+
+
+def x_sum_kernel(p0, p1, p2, p3, out):
+    out[...] = four_sum((p0, p1, p2, p3)).astype(BF)
+
+
+def y_sum_kernel(meta, p0, p1, p2, p3, grad, bias, two):
+    total = four_sum((p0, p1, p2, p3))
     half = grad.shape[1]
     grad[0] = total[:half]
     grad[1] = total[half : 2 * half]
     bias[...] = total[2 * half : 2 * half + 1]
-    two[...] = total[2 * half + 16 :]
+    n = two.shape[0]
+    rows = total[2 * half + 16 :]
+    mine = rows[:n]
+    for y in range(1, NY):
+        mine = jnp.where(meta[2] == y, rows[y * n : (y + 1) * n], mine)
+    two[...] = mine
 
 
 def all_to_all(value, axes):
@@ -273,7 +280,8 @@
     lanes = NC * feats
     per = CHIPS // STEPS
     core = lax.axis_index("core")
-    meta = jnp.full((1,), core, jnp.int32)
+    x_at, y_at = lax.axis_index("x"), lax.axis_index("grp")
+    meta = jnp.stack([core, x_at, y_at]).astype(jnp.int32)
     swap = lambda v: shift(v, "core", NC, 1)
 
     sibling = swap(local)
@@ -340,6 +348,14 @@
         self_kernel, shape((owned, width), F32), [left_spec, w_spec(0)], (feats_here, w_all),
         "self_part", us=4.0, grid=(STEPS,), out_specs=whole((owned, width)),
     )
+    def over_x(value):
+        by_x = value.reshape(NX, NZ, owned, lanes)
+        pick = lambda d: lax.dynamic_index_in_dim(by_x, (x_at + d) % NX, 0, keepdims=False)
+        return [shift(pick(d), "x", NX, d) if d else pick(0) for d in range(NX)]
+
+    lefts = over_x(mine) + over_x(means)
+    self_part, *lefts = lax.optimization_barrier((self_part, *lefts))
+
     send = send_rows[0, 0].reshape(1, -1)
     bias_row = b_one[None, :]
     ins = (self_part, bias_row, d_self, returned, send)
@@ -354,11 +370,7 @@
         us=4.0, grid=(STEPS,), out_specs=tuple(whole(o.shape) for o in outs),
     )
     d_pre_z = lax.all_gather(d_pre, "z", axis=0, tiled=True)
-    both = jnp.concatenate(
-        [mine.reshape(NX, NZ * owned, lanes), means.reshape(NX, NZ * owned, lanes)], axis=1
-    )
-    both, table = lax.optimization_barrier((both, exchange(outgoing)))
-    left = all_to_all(both, "x")
+    table = exchange(outgoing)
 
     block_rows = 2 * width // (CHIPS * NC)
     emb, two_own, two_sib = call(
@@ -372,49 +384,45 @@
         (meta, table, counts, deg_row, h_one, cot, w_two),
         "layer_two", us=3.0,
     )
-    d_pre_z, two_sib = lax.optimization_barrier((d_pre_z, two_sib))
-    two_recv = swap(two_sib)
+    two_chip = call(
+        two_sum_kernel,
+        shape((NZ, NX * block_rows, width), BF),
+        [vmem()] * 2,
+        (two_own, swap(two_sib)),
+        "two_sum",
+    )
+    d_pre_z, two_chip = lax.optimization_barrier((d_pre_z, two_chip))
+    two_z = all_to_all(two_chip, "z")
 
     rows = 2 * feats + 16
-    one_spec = pl.BlockSpec((1, rows, width), lambda i: (i, 0, 0))
     one_own, one_sib = call(
         weight_grad_kernel,
         (shape((NX, rows, width), F32), shape((NX, rows, width), F32)),
-        [
-            smem(), pl.BlockSpec((1, 2 * NZ * owned, lanes), lambda i: (i, 0, 0)),
-            whole(d_pre_z.shape),
-        ],
-        (meta, left, d_pre_z),
-        "weight_grad",
-        us=4.0, grid=(NX,), out_specs=(one_spec, one_spec),
-    )
-    one_recv = swap(one_sib)
-    two_rows = NZ * block_rows
+        [smem()] + [vmem()] * (2 * NX + 1),
+        (meta, *lefts, d_pre_z),
+        "weight_grad", us=15.0,
+    )
+    piece = shape((rows + block_rows, width), BF)
     sums = call(
         core_sum_kernel,
-        shape((NX, rows + two_rows, width), BF),
-        [vmem()] * 4,
-        (
-            one_own, one_recv, two_own.reshape(NX, two_rows, width),
-            two_recv.reshape(NX, two_rows, width),
-        ),
-        "core_sum",
-    )
-    sums = call(
-        x_sum_kernel, shape((NY, rows + two_rows // NY, width), BF), [vmem()],
-        (all_to_all(sums, "x"),), "x_sum",
-    )
-    grad_w_one, grad_b_one, two = call(
+        (piece,) * NX,
+        [smem()] + [vmem()] * 3,
+        (meta, one_own, swap(one_sib), two_z),
+        "core_sum", us=2.0,
+    )
+    got = [sums[0]] + [shift(sums[e], "x", NX, e) for e in range(1, NX)]
+    total = call(x_sum_kernel, piece, [vmem()] * NX, tuple(got), "x_sum")
+    got = [total] + [shift(total, "grp", NY, e) for e in range(1, NY)]
+    grad_w_one, grad_b_one, grad_w_two = call(
         y_sum_kernel,
         (
             shape((2, feats, width), F32), shape((1, width), F32),
-            shape((two_rows // NY, width), F32),
+            shape((block_rows // NY, width), F32),
         ),
-        [vmem()],
-        (all_to_all(sums, "grp"),),
+        [smem()] + [vmem()] * NY,
+        (meta, *got),
         "y_sum",
     )
-    grad_w_two = jnp.sum(all_to_all(two.reshape(NZ, -1, width), "z"), axis=0)
     return emb[None], grad_w_one, grad_b_one[0], grad_w_two
 
 

time: 283 us -> 266 us (0.940)
  waiting for transfers between devices: 72 us -> 37.8 us
  blocking collectives: 46.7 us -> 56.8 us
  starting transfers between devices: 51.1 us -> 55.7 us
    all_to_all x5 -> x3, waiting for transfers between devices: 52.5 us -> 2.07 us  [all_to_all(): return lax.all_to_all(value, axes, split_axis=0, concat_axis=0, tiled=True)]
    ppermute x3 -> x15, waiting for transfers between devices: 3.28 us -> 35 us  [shift(): lax.ppermute(value, axis, [(s, (s + by) % size) for s in range(size)])]
    ppermute x3 -> x15, starting transfers between devices: 0.6 us -> 20.9 us  [shift(): lax.ppermute(value, axis, [(s, (s + by) % size) for s in range(size)])]
    all_to_all x5 -> x3, starting transfers between devices: 50.4 us -> 34.8 us  [all_to_all(): return lax.all_to_all(value, axes, split_axis=0, concat_axis=0, tiled=True)]
    all_gather x1, waiting for transfers between devices: 13.2 us -> 0.01 us  [on_device(): d_pre_z = lax.all_gather(d_pre, 'z', axis=0, tiled=True)]
    all_to_all x3 -> x2, blocking collectives: 46.7 us -> 56.8 us  [all_to_all(): return lax.all_to_all(value, axes, split_axis=0, concat_axis=0, tiled=True)]
    squeeze x0 -> x2, local copies, waits for them, and re-layouts: none -> 2.99 us  [over_x(): lax.dynamic_index_in_dim(by_x, (x_at + d) % NX, 0, keepdims=False)]
    unnamed x24 -> x40, local copies, waits for them, and re-layouts: 5.88 us -> 7.52 us
  transfers between devices with their start and end apart: 10 -> 20, of which waited for: 8 -> 10; matrix products, arithmetic and copies ran while one was open for 3% -> 5% of each run, Pallas kernels for 22% -> 25%
where the time goes in v2:
time: 266 us; the launch traced here: 265 us
  Pallas kernels  82.2 us (31%)
  blocking collectives  56.8 us (21%)
  starting transfers between devices  55.7 us (21%)
  waiting for transfers between devices  37.8 us (14%)
  local copies, waits for them, and re-layouts  17.5 us (7%)
  between operations  14.3 us (5%)
    pallas_call x12, Pallas kernels, call(): pl.pallas_call(body, out_shape=outs, in_specs=ins, out_specs=jax.tree.map...  82.2 us
    all_to_all x2, blocking collectives, all_to_all(): return lax.all_to_all(value, axes, split_axis=0, concat_axis=0, tiled=True)  56.8 us
    ppermute x15, waiting for transfers between devices, shift(): lax.ppermute(value, axis, [(s, (s + by) % size) for s in range(size)])  35 us
    all_to_all x3, starting transfers between devices, all_to_all(): return lax.all_to_all(value, axes, split_axis=0, concat_axis=0, tiled=True)  34.8 us
    ppermute x15, starting transfers between devices, shift(): lax.ppermute(value, axis, [(s, (s + by) % size) for s in range(size)])  20.9 us
    unnamed x40, local copies, waits for them, and re-layouts  7.52 us
  transfers between devices with their start and end apart: 20, of which 10 were waited for; matrix products, arithmetic and copies ran while one was open for 5% of the time, Pallas kernels for 25%

profile of v2, /device:TPU:2, one launch (start us, length us, event | category | flops | bytes accessed | tf_op | source)
XLA Modules:
  0.0 264.8 jit_solution(10413774647914033512)
XLA Ops:
  9.3 3.4 %table_grad.1 = (bf16[512,512]{1,0:T(8,128)(2,1)}, f32[128,512]{1,0:T(8,128)}, bf16[512,128]{1,0:T(8,128)(2,1)}) custom-call(bf16[128,512]{1,0:T(8,128)(2,1)} %bitcast.42, bf16[1024,512]{1,0:T(8,128)(2,1)} %w_two.3, s32[1,25,128]{2,1,0:T(8,128)} %copy.17.slot, s32[1,128]{1,0:T(1,128)} %deg_row.3), custom_call_target="tpu_custom_call" | custom-call | bytes 10800000 | tf_op jit(solution)/shard_map/table_grad/pallas_call | solution.py:37
  14.8 14.8 %all-to-all-start = ((bf16[256,2,512]{2,1,0:T(2,128)(2,1)}), bf16[256,2,512]{2,1,0:T(2,128)(2,1)S(1)}, u32[]{:S(2)}, u32[]{:S(2)}) async-start(bf16[256,2,512]{2,1,0:T(2,128)(2,1)} %reshape.36), calls=%async_computation | async-start | bytes 1048576 | tf_op jit(solution)/shard_map/all_to_all | solution.py:271
  32.1 5.6 %node_table.1.refs_2_.refs_1_ = f32[8192,128]{1,0:T(8,128)} custom-call(s32[3]{0:T(128)} %pad_add_fusion.refs_0_.meta, bf16[64,8192]{1,0:T(8,128)(2,1)} %bitcast.40, bf16[64,8192]{1,0:T(8,128)(2,1)} %copy-done.6), custom_call_target="tpu_custom_call" | custom-call | bytes 21600000 | tf_op jit(solution)/shard_map/node_table/pallas_call | solution.py:37
  37.7 14.0 %mean_first.1 = (bf16[32,128,128]{2,1,0:T(8,128)(2,1)}, bf16[32,128,128]{2,1,0:T(8,128)(2,1)}) custom-call(s32[3]{0:T(128)} %pad_add_fusion.refs_0_.meta, s32[40960]{0:T(1024)} %reshape.35.refs_1_.refs_0_, f32[8192,128]{1,0:T(8,128)} %node_table.1.refs_2_.refs_1_, bf16[512,512]{1,0:T(8,128)(2,1)} %get-tuple-element.35.refs_3_), custom_call_target="tpu_custom_call" | custom-call | bytes 36864000 | tf_op jit(solution)/shard_map/mean_first/pallas_call | solution.py:37
  51.7 10.7 %all-to-all-start.2 = ((bf16[32,128,128]{2,1,0:T(8,128)(2,1)}), bf16[32,128,128]{2,1,0:T(8,128)(2,1)S(1)}, u32[]{:S(2)}, u32[]{:S(2)}) async-start(bf16[32,128,128]{2,1,0:T(8,128)(2,1)} %get-tuple-element.37), calls=%async_computation.2 | async-start | bytes 2097152 | tf_op jit(solution)/shard_map/all_to_all | solution.py:271
  63.5 32.3 %mean_last.1 = bf16[32,128,128]{2,1,0:T(8,128)(2,1)} custom-call(s32[40960]{0:T(1024)} %reshape.35.refs_1_.refs_0_, f32[8192,128]{1,0:T(8,128)} %node_table.1.refs_2_.refs_1_, bf16[32,128,128]{2,1,0:T(8,128)(2,1)} %get-tuple-element.36.refs_2_, bf16[512,512]{1,0:T(8,128)(2,1)} %reshape.37.refs_3_.returned), custom_call_target="tpu_custom_call", output_to_operand_aliasing={{}: (2, {})} | custom-call | bytes 110592000 | tf_op jit(solution)/shard_map/mean_last/pallas_call | solution.py:37
  97.9 9.2 %all-to-all-start.1 = ((bf16[32,128,128]{2,1,0:T(8,128)(2,1)}), bf16[32,128,128]{2,1,0:T(8,128)(2,1)S(1)}, u32[]{:S(2)}, u32[]{:S(2)}) async-start(bf16[32,128,128]{2,1,0:T(8,128)(2,1)} %mean_last.1), calls=%async_computation.1 | async-start | bytes 2097152 | tf_op jit(solution)/shard_map/all_to_all | solution.py:271
  111.8 2.4 collective-permute-start.3
  115.0 3.5 %collective-permute-start.5 = (bf16[8,128,128]{2,1,0:T(8,128)(2,1)S(1)}, bf16[8,128,128]{2,1,0:T(8,128)(2,1)S(1)}, u32[]{:S(2)}, u32[]{:S(2)}) collective-permute-start(bf16[8,128,128]{2,1,0:T(8,128)(2,1)S(1)} %get-tuple-element.67), channel_id=1, source_target_pairs={{0,128},{64,192},{128,0},{192,64},{1,129},{65,193},{129,1},{193,65... | collective-permute-start | bytes 786440 | tf_op jit(solution)/shard_map/ppermute | solution.py:59
  118.5 12.5 %collective-permute-done.1.refs_1_ = bf16[8,128,128]{2,1,0:T(8,128)(2,1)S(1)} collective-permute-done((bf16[8,128,128]{2,1,0:T(8,128)(2,1)S(1)}, bf16[8,128,128]{2,1,0:T(8,128)(2,1)S(1)}, u32[]{:S(2)}, u32[]{:S(2)}) %collective-permute-start.1) | collective-permute-done | bytes 262176 | tf_op jit(solution)/shard_map/ppermute | solution.py:59
  131.8 2.5 collective-permute-start.6
  135.2 4.5 %self_part.1 = f32[128,512]{1,0:T(8,128)} custom-call(bf16[32,128,128]{2,1,0:T(8,128)(2,1)} %copy-done.3, bf16[64,2,64,512]{3,2,1,0:T(8,128)(2,1)} %bitcast.35), custom_call_target="tpu_custom_call" | custom-call | bytes 14400000 | tf_op jit(solution)/shard_map/self_part/pallas_call | solution.py:37
  141.6 3.8 %collective-permute-done.6.refs_7_ = bf16[8,128,128]{2,1,0:T(8,128)(2,1)S(1)} collective-permute-done((bf16[8,128,128]{2,1,0:T(8,128)(2,1)S(1)}, bf16[8,128,128]{2,1,0:T(8,128)(2,1)S(1)}, u32[]{:S(2)}, u32[]{:S(2)}) %collective-permute-start.6) | collective-permute-done | bytes 262176 | tf_op jit(solution)/shard_map/ppermute | solution.py:59
  146.4 5.5 %node_update.1 = (bf16[128,512]{1,0:T(8,128)(2,1)}, bf16[128,512]{1,0:T(8,128)(2,1)}, bf16[512,512]{1,0:T(8,128)(2,1)}) custom-call(bf16[32,128,128]{2,1,0:T(8,128)(2,1)} %copy-done.2, bf16[64,2,64,512]{3,2,1,0:T(8,128)(2,1)} %bitcast.36, f32[128,512]{1,0:T(8,128)} %self_part.1, f32[1,512]{1,0:T(1,128)} %bitcast.45, f32[128,512]{1,0:T(8,128)} %get-tuple-element.39.d_self, ...), custom_call_target="tpu_custom_call" | custom-call | bytes 14400000 | tf_op jit(solution)/shard_map/node_update/pallas_call | solution.py:37
  153.2 35.6 %all_to_all.25 = bf16[256,2,512]{2,1,0:T(2,128)(2,1)S(1)} all-to-all(bf16[256,2,512]{2,1,0:T(2,128)(2,1)S(1)} %reshape.42), channel_id=1, replica_groups=mesh['x'=4,'z'=8,'core'=2,'grp'=4] {'x','z','core','grp'}, dimensions={0} | all-to-all | bytes 1048576 | tf_op jit(solution)/shard_map/all_to_all | solution.py:271
  189.8 3.5 %layer_two.1 = (bf16[128,512]{1,0:T(8,128)(2,1)}, f32[32,16,512]{2,1,0:T(8,128)}, bf16[32,16,512]{2,1,0:T(8,128)(2,1)}) custom-call(s32[3]{0:T(128)} %pad_add_fusion.refs_0_.meta, bf16[512,512]{1,0:T(8,128)(2,1)} %reshape.43.table, bf16[512,128]{1,0:T(8,128)(2,1)} %get-tuple-element.41.counts, s32[1,128]{1,0:T(1,128)} %deg_row.3, ...), custom_call_target="tpu_custom_call" | custom-call | bytes 10800000 | tf_op jit(solution)/shard_map/layer_two/pallas_call | solution.py:37
  196.2 2.2 two_sum.1
  198.5 4.7 %weight_grad.1 = (f32[4,144,512]{2,1,0:T(8,128)}, f32[4,144,512]{2,1,0:T(8,128)}) custom-call(s32[3]{0:T(128)} %pad_add_fusion.refs_0_.meta, bf16[8,128,128]{2,1,0:T(8,128)(2,1)} %get-tuple-element.44.refs_0_, bf16[8,128,128]{2,1,0:T(8,128)(2,1)} %copy-done.8, bf16[8,128,128]{2,1,0:T(8,128)(2,1)} %collective-permute-done.2.refs_2_, ...), custom_call_target="tpu_custom_call" | custom-call | bytes 54000000 | tf_op jit(solution)/shard_map/weight_grad/pallas_call | solution.py:37
  203.5 21.2 %all_to_all.26.two = bf16[8,64,512]{2,1,0:T(8,128)(2,1)} all-to-all(bf16[8,64,512]{2,1,0:T(8,128)(2,1)S(1)} %copy-done.4), channel_id=1, replica_groups=mesh['x'=4,'z'=8,'core'=2,'grp'=4] {'z'}, dimensions={0} | all-to-all | bytes 1048576 | tf_op jit(solution)/shard_map/all_to_all | solution.py:271
  225.7 2.6 core_sum.1
  229.8 3.4 %collective-permute-start.10 = (bf16[160,512]{1,0:T(8,128)(2,1)}, bf16[160,512]{1,0:T(8,128)(2,1)S(1)}, u32[]{:S(2)}, u32[]{:S(2)}) collective-permute-start(bf16[160,512]{1,0:T(8,128)(2,1)} %get-tuple-element.61), channel_id=1, source_target_pairs={{0,128},{64,192},{128,0},{192,64},{1,129},{65,193},{129,1},{193,65... | collective-permute-start | bytes 491528 | tf_op jit(solution)/shard_map/ppermute | solution.py:59
  233.4 3.0 %collective-permute-done.9.p1 = bf16[160,512]{1,0:T(8,128)(2,1)S(1)} collective-permute-done((bf16[160,512]{1,0:T(8,128)(2,1)}, bf16[160,512]{1,0:T(8,128)(2,1)S(1)}, u32[]{:S(2)}, u32[]{:S(2)}) %collective-permute-start.9) | collective-permute-done | bytes 163872 | tf_op jit(solution)/shard_map/ppermute | solution.py:59
  238.6 2.5 collective-permute-done.11.p3
  248.0 6.7 %collective-permute-done.12.p1 = bf16[160,512]{1,0:T(8,128)(2,1)S(1)} collective-permute-done((bf16[160,512]{1,0:T(8,128)(2,1)}, bf16[160,512]{1,0:T(8,128)(2,1)S(1)}, u32[]{:S(2)}, u32[]{:S(2)}) %collective-permute-start.12) | collective-permute-done | bytes 163872 | tf_op jit(solution)/shard_map/ppermute | solution.py:59
  (83 shorter events, 40.2 us)
Async XLA Ops:
  7.2 22.4 %copy-start = (s32[1,10,8192]{2,0,1:T(1,128)S(1)}, s32[1,10,8192]{2,0,1:T(1,128)}, u32[]{:S(2)}) copy-start(s32[1,10,8192]{2,0,1:T(1,128)} %param.10) | copy-start | bytes 983044
  7.2 128.0 %all-gather.3.cloned.1.call-start = ((), (), s32[]{:S(2)}) async-start(), calls=%async_computation.5 | async-start | bytes 8519680 | tf_op jit(solution)/shard_map/all_gather | solution.py:288
  7.9 23.2 %collective-permute-start = (bf16[64,8192]{1,0:T(8,128)(2,1)}, bf16[64,8192]{1,0:T(8,128)(2,1)S(1)}, u32[]{:S(2)}, u32[]{:S(2)}) collective-permute-start(bf16[64,8192]{1,0:T(8,128)(2,1)} %bitcast.39), channel_id=1, source_target_pairs={{0,4},{4,0},{1,5},{5,1},{2,6},{6,2},{3,7},{7,3},{8,12},{12,8},{9,1... | collective-permute-start | bytes 3145736 | tf_op jit(solution)/shard_map/ppermute | solution.py:59
  14.8 37.0 %all-to-all-start = ((bf16[256,2,512]{2,1,0:T(2,128)(2,1)}), bf16[256,2,512]{2,1,0:T(2,128)(2,1)S(1)}, u32[]{:S(2)}, u32[]{:S(2)}) async-start(bf16[256,2,512]{2,1,0:T(2,128)(2,1)} %reshape.36), calls=%async_computation | async-start | bytes 1048576 | tf_op jit(solution)/shard_map/all_to_all | solution.py:271
  51.7 46.2 %all-to-all-start.2 = ((bf16[32,128,128]{2,1,0:T(8,128)(2,1)}), bf16[32,128,128]{2,1,0:T(8,128)(2,1)S(1)}, u32[]{:S(2)}, u32[]{:S(2)}) async-start(bf16[32,128,128]{2,1,0:T(8,128)(2,1)} %get-tuple-element.37), calls=%async_computation.2 | async-start | bytes 2097152 | tf_op jit(solution)/shard_map/all_to_all | solution.py:271
  97.9 11.6 %copy-start.3 = (bf16[32,128,128]{2,1,0:T(8,128)(2,1)}, bf16[32,128,128]{2,1,0:T(8,128)(2,1)S(1)}, u32[]{:S(2)}) copy-start(bf16[32,128,128]{2,1,0:T(8,128)(2,1)S(1)} %all-to-all-done.2.left) | copy-start | bytes 3145732
  97.9 47.5 %all-to-all-start.1 = ((bf16[32,128,128]{2,1,0:T(8,128)(2,1)}), bf16[32,128,128]{2,1,0:T(8,128)(2,1)S(1)}, u32[]{:S(2)}, u32[]{:S(2)}) async-start(bf16[32,128,128]{2,1,0:T(8,128)(2,1)} %mean_last.1), calls=%async_computation.1 | async-start | bytes 2097152 | tf_op jit(solution)/shard_map/all_to_all | solution.py:271
  107.1 91.3 %all-gather.5.cloned.1.call-start = ((), (), s32[]{:S(2)}) async-start(), calls=%async_computation.6 | async-start | bytes 1179648 | tf_op jit(solution)/shard_map/all_gather | solution.py:372
  109.4 24.9 %copy-start.18 = (s32[1,1,64,4,2]{2,4,3,1,0:T(2,128)S(1)}, s32[1,1,64,4,2]{2,4,3,1,0:T(2,128)}, u32[]{:S(2)}) copy-start(s32[1,1,64,4,2]{2,4,3,1,0:T(2,128)} %param.13) | copy-start | bytes 6148
  109.4 21.6 %collective-permute-start.1 = (bf16[8,128,128]{2,1,0:T(8,128)(2,1)S(1)}, bf16[8,128,128]{2,1,0:T(8,128)(2,1)S(1)}, u32[]{:S(2)}, u32[]{:S(2)}) collective-permute-start(bf16[8,128,128]{2,1,0:T(8,128)(2,1)S(1)} %get-tuple-element.72), channel_id=1, source_target_pairs={{0,64},{64,128},{128,192},{192,0},{1,65},{65,129},{129,193},{193,1... | collective-permute-start | bytes 786440 | tf_op jit(solution)/shard_map/ppermute | solution.py:59
  110.9 28.8 %collective-permute-start.2 = (bf16[8,128,128]{2,1,0:T(8,128)(2,1)}, bf16[8,128,128]{2,1,0:T(8,128)(2,1)}, u32[]{:S(2)}, u32[]{:S(2)}) collective-permute-start(bf16[8,128,128]{2,1,0:T(8,128)(2,1)} %get-tuple-element.71), channel_id=1, source_target_pairs={{0,128},{64,192},{128,0},{192,64},{1,129},{65,193},{129,1},{193,65... | collective-permute-start | bytes 786440 | tf_op jit(solution)/shard_map/ppermute | solution.py:59
  111.8 27.9 %collective-permute-start.3 = (bf16[8,128,128]{2,1,0:T(8,128)(2,1)}, bf16[8,128,128]{2,1,0:T(8,128)(2,1)}, u32[]{:S(2)}, u32[]{:S(2)}) collective-permute-start(bf16[8,128,128]{2,1,0:T(8,128)(2,1)} %get-tuple-element.70), channel_id=1, source_target_pairs={{0,192},{64,0},{128,64},{192,128},{1,193},{65,1},{129,65},{193,129... | collective-permute-start | bytes 786440 | tf_op jit(solution)/shard_map/ppermute | solution.py:59
  115.0 24.7 %collective-permute-start.4 = (bf16[8,128,128]{2,1,0:T(8,128)(2,1)S(1)}, bf16[8,128,128]{2,1,0:T(8,128)(2,1)S(1)}, u32[]{:S(2)}, u32[]{:S(2)}) collective-permute-start(bf16[8,128,128]{2,1,0:T(8,128)(2,1)S(1)} %get-tuple-element.68), channel_id=1, source_target_pairs={{0,64},{64,128},{128,192},{192,0},{1,65},{65,129},{129,193},{193,1... | collective-permute-start | bytes 786440 | tf_op jit(solution)/shard_map/ppermute | solution.py:59
  115.0 26.6 %collective-permute-start.5 = (bf16[8,128,128]{2,1,0:T(8,128)(2,1)S(1)}, bf16[8,128,128]{2,1,0:T(8,128)(2,1)S(1)}, u32[]{:S(2)}, u32[]{:S(2)}) collective-permute-start(bf16[8,128,128]{2,1,0:T(8,128)(2,1)S(1)} %get-tuple-element.67), channel_id=1, source_target_pairs={{0,128},{64,192},{128,0},{192,64},{1,129},{65,193},{129,1},{193,65... | collective-permute-start | bytes 786440 | tf_op jit(solution)/shard_map/ppermute | solution.py:59
  131.8 13.6 %collective-permute-start.6 = (bf16[8,128,128]{2,1,0:T(8,128)(2,1)S(1)}, bf16[8,128,128]{2,1,0:T(8,128)(2,1)S(1)}, u32[]{:S(2)}, u32[]{:S(2)}) collective-permute-start(bf16[8,128,128]{2,1,0:T(8,128)(2,1)S(1)} %get-tuple-element.66), channel_id=1, source_target_pairs={{0,192},{64,0},{128,64},{192,128},{1,193},{65,1},{129,65},{193,129... | collective-permute-start | bytes 786440 | tf_op jit(solution)/shard_map/ppermute | solution.py:59
  139.7 12.1 %copy-start.9 = (bf16[8,128,128]{2,1,0:T(8,128)(2,1)}, bf16[8,128,128]{2,1,0:T(8,128)(2,1)S(1)}, u32[]{:S(2)}) copy-start(bf16[8,128,128]{2,1,0:T(8,128)(2,1)S(1)} %collective-permute-done.4.refs_5_) | copy-start | bytes 786436
  193.3 2.1 collective-permute-start.7
  203.2 21.5 %collective-permute-start.8 = (f32[4,144,512]{2,1,0:T(8,128)}, f32[4,144,512]{2,1,0:T(8,128)S(1)}, u32[]{:S(2)}, u32[]{:S(2)}) collective-permute-start(f32[4,144,512]{2,1,0:T(8,128)} %get-tuple-element.57), channel_id=1, source_target_pairs={{0,4},{4,0},{1,5},{5,1},{2,6},{6,2},{3,7},{7,3},{8,12},{12,8},{9,1... | collective-permute-start | bytes 3538952 | tf_op jit(solution)/shard_map/ppermute | solution.py:59
  228.4 8.0 %collective-permute-start.9 = (bf16[160,512]{1,0:T(8,128)(2,1)}, bf16[160,512]{1,0:T(8,128)(2,1)S(1)}, u32[]{:S(2)}, u32[]{:S(2)}) collective-permute-start(bf16[160,512]{1,0:T(8,128)(2,1)} %get-tuple-element.60), channel_id=1, source_target_pairs={{0,64},{64,128},{128,192},{192,0},{1,65},{65,129},{129,193},{193,1... | collective-permute-start | bytes 491528 | tf_op jit(solution)/shard_map/ppermute | solution.py:59
  229.8 8.8 %collective-permute-start.10 = (bf16[160,512]{1,0:T(8,128)(2,1)}, bf16[160,512]{1,0:T(8,128)(2,1)S(1)}, u32[]{:S(2)}, u32[]{:S(2)}) collective-permute-start(bf16[160,512]{1,0:T(8,128)(2,1)} %get-tuple-element.61), channel_id=1, source_target_pairs={{0,128},{64,192},{128,0},{192,64},{1,129},{65,193},{129,1},{193,65... | collective-permute-start | bytes 491528 | tf_op jit(solution)/shard_map/ppermute | solution.py:59
  233.3 7.9 %collective-permute-start.11 = (bf16[160,512]{1,0:T(8,128)(2,1)}, bf16[160,512]{1,0:T(8,128)(2,1)S(1)}, u32[]{:S(2)}, u32[]{:S(2)}) collective-permute-start(bf16[160,512]{1,0:T(8,128)(2,1)} %get-tuple-element.62), channel_id=1, source_target_pairs={{0,192},{64,0},{128,64},{192,128},{1,193},{65,1},{129,65},{193,129... | collective-permute-start | bytes 491528 | tf_op jit(solution)/shard_map/ppermute | solution.py:59
  243.7 10.9 %collective-permute-start.12 = (bf16[160,512]{1,0:T(8,128)(2,1)}, bf16[160,512]{1,0:T(8,128)(2,1)S(1)}, u32[]{:S(2)}, u32[]{:S(2)}) collective-permute-start(bf16[160,512]{1,0:T(8,128)(2,1)} %x_sum.1.p0), channel_id=1, source_target_pairs={{0,1},{1,2},{2,3},{3,0},{4,5},{5,6},{6,7},{7,4},{8,9},{9,10},{10,1... | collective-permute-start | bytes 491528 | tf_op jit(solution)/shard_map/ppermute | solution.py:59
  244.2 10.4 %collective-permute-start.13 = (bf16[160,512]{1,0:T(8,128)(2,1)}, bf16[160,512]{1,0:T(8,128)(2,1)S(1)}, u32[]{:S(2)}, u32[]{:S(2)}) collective-permute-start(bf16[160,512]{1,0:T(8,128)(2,1)} %x_sum.1.p0), channel_id=1, source_target_pairs={{0,2},{1,3},{2,0},{3,1},{4,6},{5,7},{6,4},{7,5},{8,10},{9,11},{10,... | collective-permute-start | bytes 491528 | tf_op jit(solution)/shard_map/ppermute | solution.py:59
  246.4 8.8 %collective-permute-start.14 = (bf16[160,512]{1,0:T(8,128)(2,1)}, bf16[160,512]{1,0:T(8,128)(2,1)S(1)}, u32[]{:S(2)}, u32[]{:S(2)}) collective-permute-start(bf16[160,512]{1,0:T(8,128)(2,1)} %x_sum.1.p0), channel_id=1, source_target_pairs={{0,3},{1,0},{2,1},{3,2},{4,7},{5,4},{6,5},{7,6},{8,11},{9,8},{10,9... | collective-permute-start | bytes 491528 | tf_op jit(solution)/shard_map/ppermute | solution.py:59
  (15 other events, 43.4 us)
Sparse Core Ops, SparseCore 0:
  10.8 105.2 all-gather.2
  152.0 43.1 all-gather.4

commit v3 on v2

--- a/solution.py
+++ b/solution.py
@@ -202,14 +202,6 @@
         rows = pl.ds(part * half, half)
         own[rows] = jnp.where(first, grad[:, 0], grad[:, 1])
         sib[rows] = jnp.where(first, grad[:, 1], grad[:, 0]).astype(BF)
-
-
-def two_sum_kernel(own, recv, out):
-    n = own.shape[1]
-    for x in range(NX):
-        for z in range(NZ):
-            total = own[x * NZ + z] + recv[x * NZ + z].astype(F32)
-            out[z, pl.ds(x * n, n), :] = total.astype(BF)
 
 
 def weight_grad_kernel(meta, *refs):
@@ -232,16 +224,12 @@
         sib[e, pl.ds(lanes, 16), :] = tail
 
 
-def core_sum_kernel(meta, own, recv, two, p0, p1, p2, p3):
+def core_sum_kernel(meta, own, recv, two_own, two_recv, p0, p1, p2, p3):
     rows = own.shape[1]
-    n = two.shape[1] // NX
     for e, out in enumerate((p0, p1, p2, p3)):
         out[:rows, :] = (own[e] + recv[e]).astype(BF)
-        at = pl.multiple_of(lax.rem(meta[1] + e, NX) * n, n)
-        total = two[0, pl.ds(at, n), :].astype(F32)
-        for z in range(1, NZ):
-            total = total + two[z, pl.ds(at, n), :].astype(F32)
-        out[rows:, :] = total.astype(BF)
+        x = lax.rem(meta[1] + e, NX)
+        out[rows:, :] = (two_own[x] + two_recv[x].astype(F32)).astype(BF)
 
 
 def four_sum(parts):
@@ -249,22 +237,19 @@
     return (p0 + p2) + (p1 + p3)
 
 
-def x_sum_kernel(p0, p1, p2, p3, out):
-    out[...] = four_sum((p0, p1, p2, p3)).astype(BF)
-
-
-def y_sum_kernel(meta, p0, p1, p2, p3, grad, bias, two):
+def x_sum_kernel(p0, p1, p2, p3, one, two):
+    total = four_sum((p0, p1, p2, p3)).astype(BF)
+    rows = one.shape[0]
+    one[...] = total[:rows]
+    two[...] = total[rows:]
+
+
+def y_sum_kernel(p0, p1, p2, p3, grad, bias):
     total = four_sum((p0, p1, p2, p3))
     half = grad.shape[1]
     grad[0] = total[:half]
     grad[1] = total[half : 2 * half]
     bias[...] = total[2 * half : 2 * half + 1]
-    n = two.shape[0]
-    rows = total[2 * half + 16 :]
-    mine = rows[:n]
-    for y in range(1, NY):
-        mine = jnp.where(meta[2] == y, rows[y * n : (y + 1) * n], mine)
-    two[...] = mine
 
 
 def all_to_all(value, axes):
@@ -326,7 +311,13 @@
         "mean_first", acc, us_per * FIRST_MEANS, (FIRST_MEANS,),
         (pl.BlockSpec((mean_per, owned, lanes), lambda i: (i, 0, 0)), whole(mean_shape.shape)),
     )
+    def over_x(value):
+        by_x = value.reshape(NX, NZ, owned, lanes)
+        pick = lambda d: lax.dynamic_index_in_dim(by_x, (x_at + d) % NX, 0, keepdims=False)
+        return [shift(pick(d), "x", NX, d) if d else pick(0) for d in range(NX)]
+
     feats_here = all_to_all(mine, CHIP)
+    lefts = over_x(mine)
     last = MEAN_STEPS - FIRST_MEANS
     means = call(
         lambda *refs: last_mean_kernel(fanout, *refs),
@@ -337,6 +328,7 @@
         pl.BlockSpec((mean_per, owned, lanes), lambda i: (i + FIRST_MEANS, 0, 0)),
         {2: 0},
     )
+    means, *lefts = lax.optimization_barrier((means, *lefts))
     means_here = all_to_all(means, CHIP)
 
     left_spec = pl.BlockSpec((per, owned, lanes), lambda i: (i, 0, 0))
@@ -348,12 +340,7 @@
         self_kernel, shape((owned, width), F32), [left_spec, w_spec(0)], (feats_here, w_all),
         "self_part", us=4.0, grid=(STEPS,), out_specs=whole((owned, width)),
     )
-    def over_x(value):
-        by_x = value.reshape(NX, NZ, owned, lanes)
-        pick = lambda d: lax.dynamic_index_in_dim(by_x, (x_at + d) % NX, 0, keepdims=False)
-        return [shift(pick(d), "x", NX, d) if d else pick(0) for d in range(NX)]
-
-    lefts = over_x(mine) + over_x(means)
+    lefts = lefts + over_x(means)
     self_part, *lefts = lax.optimization_barrier((self_part, *lefts))
 
     send = send_rows[0, 0].reshape(1, -1)
@@ -384,15 +371,8 @@
         (meta, table, counts, deg_row, h_one, cot, w_two),
         "layer_two", us=3.0,
     )
-    two_chip = call(
-        two_sum_kernel,
-        shape((NZ, NX * block_rows, width), BF),
-        [vmem()] * 2,
-        (two_own, swap(two_sib)),
-        "two_sum",
-    )
-    d_pre_z, two_chip = lax.optimization_barrier((d_pre_z, two_chip))
-    two_z = all_to_all(two_chip, "z")
+    d_pre_z, two_sib = lax.optimization_barrier((d_pre_z, two_sib))
+    two_recv = swap(two_sib)
 
     rows = 2 * feats + 16
     one_own, one_sib = call(
@@ -402,25 +382,30 @@
         (meta, *lefts, d_pre_z),
         "weight_grad", us=15.0,
     )
-    piece = shape((rows + block_rows, width), BF)
+    two_rows = NZ * block_rows
     sums = call(
         core_sum_kernel,
-        (piece,) * NX,
-        [smem()] + [vmem()] * 3,
-        (meta, one_own, swap(one_sib), two_z),
+        (shape((rows + two_rows, width), BF),) * NX,
+        [smem()] + [vmem()] * 4,
+        (
+            meta, one_own, swap(one_sib), two_own.reshape(NX, two_rows, width),
+            two_recv.reshape(NX, two_rows, width),
+        ),
         "core_sum", us=2.0,
     )
     got = [sums[0]] + [shift(sums[e], "x", NX, e) for e in range(1, NX)]
-    total = call(x_sum_kernel, piece, [vmem()] * NX, tuple(got), "x_sum")
+    total, two = call(
+        x_sum_kernel, (shape((rows, width), BF), shape((two_rows, width), BF)), [vmem()] * NX,
+        tuple(got), "x_sum",
+    )
+    two_last = all_to_all(two.reshape(NZ * NY, -1, width), ("z", "grp"))
+    grad_w_two = jnp.sum(two_last.astype(F32), axis=0)
     got = [total] + [shift(total, "grp", NY, e) for e in range(1, NY)]
-    grad_w_one, grad_b_one, grad_w_two = call(
+    grad_w_one, grad_b_one = call(
         y_sum_kernel,
-        (
-            shape((2, feats, width), F32), shape((1, width), F32),
-            shape((block_rows // NY, width), F32),
-        ),
-        [smem()] + [vmem()] * NY,
-        (meta, *got),
+        (shape((2, feats, width), F32), shape((1, width), F32)),
+        [vmem()] * NY,
+        tuple(got),
         "y_sum",
     )
     return emb[None], grad_w_one, grad_b_one[0], grad_w_two

time: 266 us -> 252 us (0.947)
  blocking collectives: 56.8 us -> 35.5 us
  starting transfers between devices: 55.7 us -> 62 us
    all_to_all x2 -> x1, blocking collectives: 56.8 us -> 35.5 us  [all_to_all(): return lax.all_to_all(value, axes, split_axis=0, concat_axis=0, tiled=True)]
    all_to_all x3 -> x4, starting transfers between devices: 34.8 us -> 41.8 us  [all_to_all(): return lax.all_to_all(value, axes, split_axis=0, concat_axis=0, tiled=True)]
    pallas_call x12 -> x11, Pallas kernels: 82.2 us -> 80.5 us  [call(): pl.pallas_call(body, out_shape=outs, in_specs=ins, out_specs=jax.tree.map...]
    unnamed x40 -> x46, local copies, waits for them, and re-layouts: 7.52 us -> 7.46 us
  transfers between devices with their start and end apart: 20 -> 21, of which waited for: 10 -> 11; matrix products, arithmetic and copies ran while one was open for 5% -> 4% of each run, Pallas kernels for 25% -> 26%
where the time goes in v3:
time: 252 us; the launch traced here: 251 us
  Pallas kernels  80.5 us (32%)
  starting transfers between devices  62 us (25%)
  waiting for transfers between devices  38.8 us (15%)
  blocking collectives  35.5 us (14%)
  local copies, waits for them, and re-layouts  18.1 us (7%)
  between operations  14.3 us (6%)
    pallas_call x11, Pallas kernels, call(): pl.pallas_call(body, out_shape=outs, in_specs=ins, out_specs=jax.tree.map...  80.5 us
    all_to_all x4, starting transfers between devices, all_to_all(): return lax.all_to_all(value, axes, split_axis=0, concat_axis=0, tiled=True)  41.8 us
    ppermute x15, waiting for transfers between devices, shift(): lax.ppermute(value, axis, [(s, (s + by) % size) for s in range(size)])  35.7 us
    all_to_all x1, blocking collectives, all_to_all(): return lax.all_to_all(value, axes, split_axis=0, concat_axis=0, tiled=True)  35.5 us
    ppermute x15, starting transfers between devices, shift(): lax.ppermute(value, axis, [(s, (s + by) % size) for s in range(size)])  20.2 us
    unnamed x46, local copies, waits for them, and re-layouts  7.46 us
  transfers between devices with their start and end apart: 21, of which 11 were waited for; matrix products, arithmetic and copies ran while one was open for 4% of the time, Pallas kernels for 26%

profile of v3, /device:TPU:2, one launch (start us, length us, event | category | flops | bytes accessed | tf_op | source)
XLA Modules:
  0.0 250.6 jit_solution(1404109952024755338)
XLA Ops:
  9.3 3.4 %table_grad.1 = (bf16[512,512]{1,0:T(8,128)(2,1)}, f32[128,512]{1,0:T(8,128)}, bf16[512,128]{1,0:T(8,128)(2,1)}) custom-call(bf16[128,512]{1,0:T(8,128)(2,1)} %bitcast.46, bf16[1024,512]{1,0:T(8,128)(2,1)} %w_two.3, s32[1,25,128]{2,1,0:T(8,128)} %copy.17.slot, s32[1,128]{1,0:T(1,128)} %deg_row.3), custom_call_target="tpu_custom_call" | custom-call | bytes 10800000 | tf_op jit(solution)/shard_map/table_grad/pallas_call | solution.py:37
  14.8 14.8 %all-to-all-start = ((bf16[256,2,512]{2,1,0:T(2,128)(2,1)}), bf16[256,2,512]{2,1,0:T(2,128)(2,1)S(1)}, u32[]{:S(2)}, u32[]{:S(2)}) async-start(bf16[256,2,512]{2,1,0:T(2,128)(2,1)} %reshape.45), calls=%async_computation | async-start | bytes 1048576 | tf_op jit(solution)/shard_map/all_to_all | solution.py:256
  32.2 5.6 %node_table.1.refs_2_.refs_1_ = f32[8192,128]{1,0:T(8,128)} custom-call(s32[3]{0:T(128)} %pad_add_fusion.refs_0_.meta, bf16[64,8192]{1,0:T(8,128)(2,1)} %bitcast.42, bf16[64,8192]{1,0:T(8,128)(2,1)} %copy-done.6), custom_call_target="tpu_custom_call" | custom-call | bytes 21600000 | tf_op jit(solution)/shard_map/node_table/pallas_call | solution.py:37
  37.8 14.0 %mean_first.1 = (bf16[32,128,128]{2,1,0:T(8,128)(2,1)}, bf16[32,128,128]{2,1,0:T(8,128)(2,1)}) custom-call(s32[3]{0:T(128)} %pad_add_fusion.refs_0_.meta, s32[40960]{0:T(1024)} %reshape.44.refs_1_.refs_0_, f32[8192,128]{1,0:T(8,128)} %node_table.1.refs_2_.refs_1_, bf16[512,512]{1,0:T(8,128)(2,1)} %get-tuple-element.41.refs_3_), custom_call_target="tpu_custom_call" | custom-call | bytes 36864000 | tf_op jit(solution)/shard_map/mean_first/pallas_call | solution.py:37
  51.8 10.9 %all-to-all-start.2 = ((bf16[32,128,128]{2,1,0:T(8,128)(2,1)}), bf16[32,128,128]{2,1,0:T(8,128)(2,1)S(1)}, u32[]{:S(2)}, u32[]{:S(2)}) async-start(bf16[32,128,128]{2,1,0:T(8,128)(2,1)} %get-tuple-element.43), calls=%async_computation.2 | async-start | bytes 2097152 | tf_op jit(solution)/shard_map/all_to_all | solution.py:256
  66.1 2.4 collective-permute-start.3
  69.5 32.3 %mean_last.1 = bf16[32,128,128]{2,1,0:T(8,128)(2,1)} custom-call(s32[40960]{0:T(1024)} %reshape.44.refs_1_.refs_0_, f32[8192,128]{1,0:T(8,128)} %node_table.1.refs_2_.refs_1_, bf16[32,128,128]{2,1,0:T(8,128)(2,1)} %get-tuple-element.42.refs_2_, bf16[512,512]{1,0:T(8,128)(2,1)} %reshape.46.refs_3_.returned), custom_call_target="tpu_custom_call", output_to_operand_aliasing={{}: (2, {})} | custom-call | bytes 110592000 | tf_op jit(solution)/shard_map/mean_last/pallas_call | solution.py:37
  102.7 8.4 %all-to-all-start.1 = ((bf16[32,128,128]{2,1,0:T(8,128)(2,1)}), bf16[32,128,128]{2,1,0:T(8,128)(2,1)S(1)}, u32[]{:S(2)}, u32[]{:S(2)}) async-start(bf16[32,128,128]{2,1,0:T(8,128)(2,1)} %mean_last.1), calls=%async_computation.1 | async-start | bytes 2097152 | tf_op jit(solution)/shard_map/all_to_all | solution.py:256
  114.6 2.4 collective-permute-start.6
  118.5 4.5 %self_part.1 = f32[128,512]{1,0:T(8,128)} custom-call(bf16[32,128,128]{2,1,0:T(8,128)(2,1)} %copy-done.2, bf16[64,2,64,512]{3,2,1,0:T(8,128)(2,1)} %bitcast.37), custom_call_target="tpu_custom_call" | custom-call | bytes 14400000 | tf_op jit(solution)/shard_map/self_part/pallas_call | solution.py:37
  123.0 3.5 %collective-permute-done.4.refs_5_ = bf16[8,128,128]{2,1,0:T(8,128)(2,1)S(1)} collective-permute-done((bf16[8,128,128]{2,1,0:T(8,128)(2,1)}, bf16[8,128,128]{2,1,0:T(8,128)(2,1)S(1)}, u32[]{:S(2)}, u32[]{:S(2)}) %collective-permute-start.4) | collective-permute-done | bytes 262176 | tf_op jit(solution)/shard_map/ppermute | solution.py:59
  126.5 5.4 %collective-permute-done.5.refs_6_ = bf16[8,128,128]{2,1,0:T(8,128)(2,1)S(1)} collective-permute-done((bf16[8,128,128]{2,1,0:T(8,128)(2,1)}, bf16[8,128,128]{2,1,0:T(8,128)(2,1)S(1)}, u32[]{:S(2)}, u32[]{:S(2)}) %collective-permute-start.5) | collective-permute-done | bytes 262176 | tf_op jit(solution)/shard_map/ppermute | solution.py:59
  131.9 4.8 %collective-permute-done.6.refs_7_ = bf16[8,128,128]{2,1,0:T(8,128)(2,1)S(1)} collective-permute-done((bf16[8,128,128]{2,1,0:T(8,128)(2,1)}, bf16[8,128,128]{2,1,0:T(8,128)(2,1)S(1)}, u32[]{:S(2)}, u32[]{:S(2)}) %collective-permute-start.6) | collective-permute-done | bytes 262176 | tf_op jit(solution)/shard_map/ppermute | solution.py:59
  137.7 5.5 %node_update.1 = (bf16[128,512]{1,0:T(8,128)(2,1)}, bf16[128,512]{1,0:T(8,128)(2,1)}, bf16[512,512]{1,0:T(8,128)(2,1)}) custom-call(bf16[32,128,128]{2,1,0:T(8,128)(2,1)} %copy-done.3, bf16[64,2,64,512]{3,2,1,0:T(8,128)(2,1)} %bitcast.38, f32[128,512]{1,0:T(8,128)} %self_part.1, f32[1,512]{1,0:T(1,128)} %bitcast.49, f32[128,512]{1,0:T(8,128)} %get-tuple-element.50.d_self, ...), custom_call_target="tpu_custom_call" | custom-call | bytes 14400000 | tf_op jit(solution)/shard_map/node_update/pallas_call | solution.py:37
  144.4 35.5 %all_to_all.25 = bf16[256,2,512]{2,1,0:T(2,128)(2,1)S(1)} all-to-all(bf16[256,2,512]{2,1,0:T(2,128)(2,1)S(1)} %reshape.51), channel_id=1, replica_groups=mesh['x'=4,'z'=8,'core'=2,'grp'=4] {'x','z','core','grp'}, dimensions={0} | all-to-all | bytes 1048576 | tf_op jit(solution)/shard_map/all_to_all | solution.py:256
  180.9 3.6 %layer_two.1 = (bf16[128,512]{1,0:T(8,128)(2,1)}, f32[32,16,512]{2,1,0:T(8,128)}, bf16[32,16,512]{2,1,0:T(8,128)(2,1)}) custom-call(s32[3]{0:T(128)} %pad_add_fusion.refs_0_.meta, bf16[512,512]{1,0:T(8,128)(2,1)} %reshape.52.table, bf16[512,128]{1,0:T(8,128)(2,1)} %get-tuple-element.52.counts, s32[1,128]{1,0:T(1,128)} %deg_row.3, ...), custom_call_target="tpu_custom_call" | custom-call | bytes 10800000 | tf_op jit(solution)/shard_map/layer_two/pallas_call | solution.py:37
  186.3 4.7 %weight_grad.1 = (f32[4,144,512]{2,1,0:T(8,128)}, f32[4,144,512]{2,1,0:T(8,128)}) custom-call(s32[3]{0:T(128)} %pad_add_fusion.refs_0_.meta, bf16[8,128,128]{2,1,0:T(8,128)(2,1)} %get-tuple-element.55.refs_0_, bf16[8,128,128]{2,1,0:T(8,128)(2,1)} %copy-done.11, bf16[8,128,128]{2,1,0:T(8,128)(2,1)} %copy-done.12, bf16[8,128,128]{2,1,0:T(8,128)(2,1)} %copy-done.13, ...), custom_call_target="tpu_custom_call" | custom-call | bytes 54000000 | tf_op jit(solution)/shard_map/weight_grad/pallas_call | solution.py:37
  191.5 3.1 %collective-permute-done.8 = bf16[32,16,512]{2,1,0:T(8,128)(2,1)S(1)} collective-permute-done((bf16[32,16,512]{2,1,0:T(8,128)(2,1)S(1)}, bf16[32,16,512]{2,1,0:T(8,128)(2,1)S(1)}, u32[]{:S(2)}, u32[]{:S(2)}) %collective-permute-start.8) | collective-permute-done | bytes 524320 | tf_op jit(solution)/shard_map/ppermute | solution.py:59
  195.8 3.2 %core_sum.1 = (bf16[272,512]{1,0:T(8,128)(2,1)}, bf16[272,512]{1,0:T(8,128)(2,1)}, bf16[272,512]{1,0:T(8,128)(2,1)}, bf16[272,512]{1,0:T(8,128)(2,1)}) custom-call(s32[3]{0:T(128)} %pad_add_fusion.refs_0_.meta, f32[4,144,512]{2,1,0:T(8,128)} %get-tuple-element.66.own, f32[4,144,512]{2,1,0:T(8,128)} %copy-done.5, f32[4,128,512]{2,1,0:T(8,128)} %bitcast.44, ...), custom_call_target="tpu_custom_call" | custom-call | bytes 7200000 | tf_op jit(solution)/shard_map/core_sum/pallas_call | solution.py:37
  203.1 7.2 %collective-permute-done.10.p2 = bf16[272,512]{1,0:T(8,128)(2,1)S(1)} collective-permute-done((bf16[272,512]{1,0:T(8,128)(2,1)}, bf16[272,512]{1,0:T(8,128)(2,1)S(1)}, u32[]{:S(2)}, u32[]{:S(2)}) %collective-permute-start.10) | collective-permute-done | bytes 278560 | tf_op jit(solution)/shard_map/ppermute | solution.py:59
  210.3 5.1 %collective-permute-done.11.p3 = bf16[272,512]{1,0:T(8,128)(2,1)S(1)} collective-permute-done((bf16[272,512]{1,0:T(8,128)(2,1)}, bf16[272,512]{1,0:T(8,128)(2,1)S(1)}, u32[]{:S(2)}, u32[]{:S(2)}) %collective-permute-start.11) | collective-permute-done | bytes 278560 | tf_op jit(solution)/shard_map/ppermute | solution.py:59
  219.8 7.7 %all-to-all-start.4 = ((bf16[32,4,512]{2,1,0:T(4,128)(2,1)}), bf16[32,4,512]{2,1,0:T(4,128)(2,1)S(1)}, u32[]{:S(2)}, u32[]{:S(2)}) async-start(bf16[32,4,512]{2,1,0:T(4,128)(2,1)} %reshape.55), calls=%async_computation.4 | async-start | bytes 262144 | tf_op jit(solution)/shard_map/all_to_all | solution.py:256
  229.4 2.7 %collective-permute-start.13 = (bf16[144,512]{1,0:T(8,128)(2,1)}, bf16[144,512]{1,0:T(8,128)(2,1)S(1)}, u32[]{:S(2)}, u32[]{:S(2)}) collective-permute-start(bf16[144,512]{1,0:T(8,128)(2,1)} %get-tuple-element.74.p0), channel_id=1, source_target_pairs={{0,2},{1,3},{2,0},{3,1},{4,6},{5,7},{6,4},{7,5},{8,10},{9,11},{10,... | collective-permute-start | bytes 442376 | tf_op jit(solution)/shard_map/ppermute | solution.py:59
  235.8 4.1 %collective-permute-done.13.p2 = bf16[144,512]{1,0:T(8,128)(2,1)S(1)} collective-permute-done((bf16[144,512]{1,0:T(8,128)(2,1)}, bf16[144,512]{1,0:T(8,128)(2,1)S(1)}, u32[]{:S(2)}, u32[]{:S(2)}) %collective-permute-start.13) | collective-permute-done | bytes 147488 | tf_op jit(solution)/shard_map/ppermute | solution.py:59
  (91 shorter events, 41.7 us)
Async XLA Ops:
  7.2 22.4 %copy-start = (s32[1,10,8192]{2,0,1:T(1,128)S(1)}, s32[1,10,8192]{2,0,1:T(1,128)}, u32[]{:S(2)}) copy-start(s32[1,10,8192]{2,0,1:T(1,128)} %param.10) | copy-start | bytes 983044
  7.2 111.3 %all-gather.3.cloned.1.call-start = ((), (), s32[]{:S(2)}) async-start(), calls=%async_computation.5 | async-start | bytes 8519680 | tf_op jit(solution)/shard_map/all_gather | solution.py:273
  7.9 23.3 %collective-permute-start = (bf16[64,8192]{1,0:T(8,128)(2,1)}, bf16[64,8192]{1,0:T(8,128)(2,1)S(1)}, u32[]{:S(2)}, u32[]{:S(2)}) collective-permute-start(bf16[64,8192]{1,0:T(8,128)(2,1)} %bitcast.41), channel_id=1, source_target_pairs={{0,4},{4,0},{1,5},{5,1},{2,6},{6,2},{3,7},{7,3},{8,12},{12,8},{9,1... | collective-permute-start | bytes 3145736 | tf_op jit(solution)/shard_map/ppermute | solution.py:59
  14.8 37.0 %all-to-all-start = ((bf16[256,2,512]{2,1,0:T(2,128)(2,1)}), bf16[256,2,512]{2,1,0:T(2,128)(2,1)S(1)}, u32[]{:S(2)}, u32[]{:S(2)}) async-start(bf16[256,2,512]{2,1,0:T(2,128)(2,1)} %reshape.45), calls=%async_computation | async-start | bytes 1048576 | tf_op jit(solution)/shard_map/all_to_all | solution.py:256
  51.8 50.1 %all-to-all-start.2 = ((bf16[32,128,128]{2,1,0:T(8,128)(2,1)}), bf16[32,128,128]{2,1,0:T(8,128)(2,1)S(1)}, u32[]{:S(2)}, u32[]{:S(2)}) async-start(bf16[32,128,128]{2,1,0:T(8,128)(2,1)} %get-tuple-element.43), calls=%async_computation.2 | async-start | bytes 2097152 | tf_op jit(solution)/shard_map/all_to_all | solution.py:256
  63.8 38.1 %collective-permute-start.1 = (bf16[8,128,128]{2,1,0:T(8,128)(2,1)}, bf16[8,128,128]{2,1,0:T(8,128)(2,1)S(1)}, u32[]{:S(2)}, u32[]{:S(2)}) collective-permute-start(bf16[8,128,128]{2,1,0:T(8,128)(2,1)} %get-tuple-element.84), channel_id=1, source_target_pairs={{0,64},{64,128},{128,192},{192,0},{1,65},{65,129},{129,193},{193,1... | collective-permute-start | bytes 786440 | tf_op jit(solution)/shard_map/ppermute | solution.py:59
  65.2 36.6 %collective-permute-start.2 = (bf16[8,128,128]{2,1,0:T(8,128)(2,1)}, bf16[8,128,128]{2,1,0:T(8,128)(2,1)S(1)}, u32[]{:S(2)}, u32[]{:S(2)}) collective-permute-start(bf16[8,128,128]{2,1,0:T(8,128)(2,1)} %get-tuple-element.83), channel_id=1, source_target_pairs={{0,128},{64,192},{128,0},{192,64},{1,129},{65,193},{129,1},{193,65... | collective-permute-start | bytes 786440 | tf_op jit(solution)/shard_map/ppermute | solution.py:59
  66.1 35.8 %collective-permute-start.3 = (bf16[8,128,128]{2,1,0:T(8,128)(2,1)}, bf16[8,128,128]{2,1,0:T(8,128)(2,1)S(1)}, u32[]{:S(2)}, u32[]{:S(2)}) collective-permute-start(bf16[8,128,128]{2,1,0:T(8,128)(2,1)} %get-tuple-element.82), channel_id=1, source_target_pairs={{0,192},{64,0},{128,64},{192,128},{1,193},{65,1},{129,65},{193,129... | collective-permute-start | bytes 786440 | tf_op jit(solution)/shard_map/ppermute | solution.py:59
  102.7 33.9 %all-to-all-start.1 = ((bf16[32,128,128]{2,1,0:T(8,128)(2,1)}), bf16[32,128,128]{2,1,0:T(8,128)(2,1)S(1)}, u32[]{:S(2)}, u32[]{:S(2)}) async-start(bf16[32,128,128]{2,1,0:T(8,128)(2,1)} %mean_last.1), calls=%async_computation.1 | async-start | bytes 2097152 | tf_op jit(solution)/shard_map/all_to_all | solution.py:256
  111.2 75.1 %all-gather.5.cloned.1.call-start = ((), (), s32[]{:S(2)}) async-start(), calls=%async_computation.6 | async-start | bytes 1179648 | tf_op jit(solution)/shard_map/all_gather | solution.py:359
  112.3 14.2 %collective-permute-start.4 = (bf16[8,128,128]{2,1,0:T(8,128)(2,1)}, bf16[8,128,128]{2,1,0:T(8,128)(2,1)S(1)}, u32[]{:S(2)}, u32[]{:S(2)}) collective-permute-start(bf16[8,128,128]{2,1,0:T(8,128)(2,1)} %get-tuple-element.80), channel_id=1, source_target_pairs={{0,64},{64,128},{128,192},{192,0},{1,65},{65,129},{129,193},{193,1... | collective-permute-start | bytes 786440 | tf_op jit(solution)/shard_map/ppermute | solution.py:59
  113.7 18.2 %collective-permute-start.5 = (bf16[8,128,128]{2,1,0:T(8,128)(2,1)}, bf16[8,128,128]{2,1,0:T(8,128)(2,1)S(1)}, u32[]{:S(2)}, u32[]{:S(2)}) collective-permute-start(bf16[8,128,128]{2,1,0:T(8,128)(2,1)} %get-tuple-element.79), channel_id=1, source_target_pairs={{0,128},{64,192},{128,0},{192,64},{1,129},{65,193},{129,1},{193,65... | collective-permute-start | bytes 786440 | tf_op jit(solution)/shard_map/ppermute | solution.py:59
  114.6 22.1 %collective-permute-start.6 = (bf16[8,128,128]{2,1,0:T(8,128)(2,1)}, bf16[8,128,128]{2,1,0:T(8,128)(2,1)S(1)}, u32[]{:S(2)}, u32[]{:S(2)}) collective-permute-start(bf16[8,128,128]{2,1,0:T(8,128)(2,1)} %get-tuple-element.78), channel_id=1, source_target_pairs={{0,192},{64,0},{128,64},{192,128},{1,193},{65,1},{129,65},{193,129... | collective-permute-start | bytes 786440 | tf_op jit(solution)/shard_map/ppermute | solution.py:59
  126.5 16.6 %copy-start.14 = (bf16[8,128,128]{2,1,0:T(8,128)(2,1)}, bf16[8,128,128]{2,1,0:T(8,128)(2,1)S(1)}, u32[]{:S(2)}) copy-start(bf16[8,128,128]{2,1,0:T(8,128)(2,1)S(1)} %collective-permute-done.4.refs_5_) | copy-start | bytes 786436
  131.9 11.2 %copy-start.15 = (bf16[8,128,128]{2,1,0:T(8,128)(2,1)}, bf16[8,128,128]{2,1,0:T(8,128)(2,1)S(1)}, u32[]{:S(2)}) copy-start(bf16[8,128,128]{2,1,0:T(8,128)(2,1)S(1)} %collective-permute-done.5.refs_6_) | copy-start | bytes 786436
  191.0 3.8 %collective-permute-start.7 = (f32[4,144,512]{2,1,0:T(8,128)}, f32[4,144,512]{2,1,0:T(8,128)S(1)}, u32[]{:S(2)}, u32[]{:S(2)}) collective-permute-start(f32[4,144,512]{2,1,0:T(8,128)} %get-tuple-element.67), channel_id=1, source_target_pairs={{0,4},{4,0},{1,5},{5,1},{2,6},{6,2},{3,7},{7,3},{8,12},{12,8},{9,1... | collective-permute-start | bytes 3538952 | tf_op jit(solution)/shard_map/ppermute | solution.py:59
  191.0 3.6 %collective-permute-start.8 = (bf16[32,16,512]{2,1,0:T(8,128)(2,1)S(1)}, bf16[32,16,512]{2,1,0:T(8,128)(2,1)S(1)}, u32[]{:S(2)}, u32[]{:S(2)}) collective-permute-start(bf16[32,16,512]{2,1,0:T(8,128)(2,1)S(1)} %copy-done.21), channel_id=1, source_target_pairs={{0,4},{4,0},{1,5},{5,1},{2,6},{6,2},{3,7},{7,3},{8,12},{12,8},{9,1... | collective-permute-start | bytes 1572872 | tf_op jit(solution)/shard_map/ppermute | solution.py:59
  199.0 11.3 %collective-permute-start.10 = (bf16[272,512]{1,0:T(8,128)(2,1)}, bf16[272,512]{1,0:T(8,128)(2,1)S(1)}, u32[]{:S(2)}, u32[]{:S(2)}) collective-permute-start(bf16[272,512]{1,0:T(8,128)(2,1)} %get-tuple-element.72), channel_id=1, source_target_pairs={{0,128},{64,192},{128,0},{192,64},{1,129},{65,193},{129,1},{193,65... | collective-permute-start | bytes 835592 | tf_op jit(solution)/shard_map/ppermute | solution.py:59
  201.0 14.3 %collective-permute-start.11 = (bf16[272,512]{1,0:T(8,128)(2,1)}, bf16[272,512]{1,0:T(8,128)(2,1)S(1)}, u32[]{:S(2)}, u32[]{:S(2)}) collective-permute-start(bf16[272,512]{1,0:T(8,128)(2,1)} %get-tuple-element.73), channel_id=1, source_target_pairs={{0,192},{64,0},{128,64},{192,128},{1,193},{65,1},{129,65},{193,129... | collective-permute-start | bytes 835592 | tf_op jit(solution)/shard_map/ppermute | solution.py:59
  202.4 13.0 %collective-permute-start.9 = (bf16[272,512]{1,0:T(8,128)(2,1)}, bf16[272,512]{1,0:T(8,128)(2,1)S(1)}, u32[]{:S(2)}, u32[]{:S(2)}) collective-permute-start(bf16[272,512]{1,0:T(8,128)(2,1)} %get-tuple-element.71), channel_id=1, source_target_pairs={{0,64},{64,128},{128,192},{192,0},{1,65},{65,129},{129,193},{193,1... | collective-permute-start | bytes 835592 | tf_op jit(solution)/shard_map/ppermute | solution.py:59
  219.8 23.3 %all-to-all-start.4 = ((bf16[32,4,512]{2,1,0:T(4,128)(2,1)}), bf16[32,4,512]{2,1,0:T(4,128)(2,1)S(1)}, u32[]{:S(2)}, u32[]{:S(2)}) async-start(bf16[32,4,512]{2,1,0:T(4,128)(2,1)} %reshape.55), calls=%async_computation.4 | async-start | bytes 262144 | tf_op jit(solution)/shard_map/all_to_all | solution.py:256
  227.5 8.3 %collective-permute-start.12 = (bf16[144,512]{1,0:T(8,128)(2,1)}, bf16[144,512]{1,0:T(8,128)(2,1)S(1)}, u32[]{:S(2)}, u32[]{:S(2)}) collective-permute-start(bf16[144,512]{1,0:T(8,128)(2,1)} %get-tuple-element.74.p0), channel_id=1, source_target_pairs={{0,1},{1,2},{2,3},{3,0},{4,5},{5,6},{6,7},{7,4},{8,9},{9,10},{10,1... | collective-permute-start | bytes 442376 | tf_op jit(solution)/shard_map/ppermute | solution.py:59
  229.4 10.5 %collective-permute-start.13 = (bf16[144,512]{1,0:T(8,128)(2,1)}, bf16[144,512]{1,0:T(8,128)(2,1)S(1)}, u32[]{:S(2)}, u32[]{:S(2)}) collective-permute-start(bf16[144,512]{1,0:T(8,128)(2,1)} %get-tuple-element.74.p0), channel_id=1, source_target_pairs={{0,2},{1,3},{2,0},{3,1},{4,6},{5,7},{6,4},{7,5},{8,10},{9,11},{10,... | collective-permute-start | bytes 442376 | tf_op jit(solution)/shard_map/ppermute | solution.py:59
  232.0 7.9 %collective-permute-start.14 = (bf16[144,512]{1,0:T(8,128)(2,1)}, bf16[144,512]{1,0:T(8,128)(2,1)S(1)}, u32[]{:S(2)}, u32[]{:S(2)}) collective-permute-start(bf16[144,512]{1,0:T(8,128)(2,1)} %get-tuple-element.74.p0), channel_id=1, source_target_pairs={{0,3},{1,0},{2,1},{3,2},{4,7},{5,4},{6,5},{7,6},{8,11},{9,8},{10,9... | collective-permute-start | bytes 442376 | tf_op jit(solution)/shard_map/ppermute | solution.py:59
  (19 other events, 66.0 us)
Sparse Core Ops, SparseCore 0:
  10.8 107.6 all-gather.2
  143.3 42.9 all-gather.4

commit v4 on v3

--- a/solution.py
+++ b/solution.py
@@ -11,7 +11,7 @@
 CHIPS = NX * NZ
 STEPS = 4
 MEAN_STEPS = 8
-FIRST_MEANS = 2
+FIRST_MEANS = 3
 FEAT = ("x", "z", "core")
 CHIP = ("x", "z")
 ALL = ("x", "z", "core", "grp")
@@ -63,8 +63,7 @@
     return lax.dot_general(a, b, (((ca,), (cb,)), ((), ())), preferred_element_type=F32)
 
 
-def table_kernel(owned, meta, own, sib, tbl):
-    core = meta[0]
+def make_table(owned, core, own, sib, tbl):
     first = core == 0
     def step(chip, carry):
         for c in range(NC):
@@ -114,9 +113,10 @@
     lax.fori_loop(0, per, chunk, 0)
 
 
-def first_mean_kernel(fanout, meta, idx, tbl, after, out, mine, acc):
+def first_mean_kernel(fanout, meta, idx, own, sib, after, out, mine, tbl, acc):
     @pl.when(pl.program_id(0) == 0)
     def _():
+        make_table(mine.shape[1], meta[0], own, sib, tbl)
         own_rows(meta[0], tbl, mine)
 
     mean_rows(fanout, 0, idx, tbl, out, acc)
@@ -238,10 +238,12 @@
 
 
 def x_sum_kernel(p0, p1, p2, p3, one, two):
-    total = four_sum((p0, p1, p2, p3)).astype(BF)
+    total = four_sum((p0, p1, p2, p3))
     rows = one.shape[0]
-    one[...] = total[:rows]
-    two[...] = total[rows:]
+    one[...] = total[:rows].astype(BF)
+    n = two.shape[1]
+    for i in range(two.shape[0]):
+        two[i] = total[rows + i * n : rows + (i + 1) * n]
 
 
 def y_sum_kernel(p0, p1, p2, p3, grad, bias):
@@ -289,13 +291,6 @@
 
     returned = exchange(d_table)
 
-    tbl = call(
-        lambda *refs: table_kernel(owned, *refs),
-        shape((group_nodes, lanes), F32),
-        [smem(), vmem(), vmem()],
-        (meta, local, sibling),
-        "node_table", us=6.0,
-    )
     by_device = nbr_one[0].reshape(fanout, CHIPS, NC, owned)
     idx = lax.dynamic_index_in_dim(by_device, core, 2, keepdims=False)
     idx = idx.transpose(1, 0, 2).reshape(-1)
@@ -303,13 +298,17 @@
     mean_per = CHIPS // MEAN_STEPS
     acc = [pltpu.VMEM((owned, lanes), F32)]
     us_per = idx.shape[0] * 1e-3 / MEAN_STEPS
-    begun, mine = call(
+    table_shape = shape((group_nodes, lanes), F32)
+    begun, mine, tbl = call(
         lambda *refs: first_mean_kernel(fanout, *refs),
-        (mean_shape, mean_shape),
-        [smem(), smem(), whole(tbl.shape), unread()],
-        (meta, idx, tbl, d_table),
-        "mean_first", acc, us_per * FIRST_MEANS, (FIRST_MEANS,),
-        (pl.BlockSpec((mean_per, owned, lanes), lambda i: (i, 0, 0)), whole(mean_shape.shape)),
+        (mean_shape, mean_shape, table_shape),
+        [smem(), smem(), whole(local.shape), whole(local.shape), unread()],
+        (meta, idx, local, sibling, d_table),
+        "mean_first", acc, us_per * FIRST_MEANS + 5.0, (FIRST_MEANS,),
+        (
+            pl.BlockSpec((mean_per, owned, lanes), lambda i: (i, 0, 0)),
+            whole(mean_shape.shape), whole(table_shape.shape),
+        ),
     )
     def over_x(value):
         by_x = value.reshape(NX, NZ, owned, lanes)
@@ -395,11 +394,11 @@
     )
     got = [sums[0]] + [shift(sums[e], "x", NX, e) for e in range(1, NX)]
     total, two = call(
-        x_sum_kernel, (shape((rows, width), BF), shape((two_rows, width), BF)), [vmem()] * NX,
+        x_sum_kernel, (shape((rows, width), BF), shape((NZ * NY, block_rows // NY, width), F32)),
+        [vmem()] * NX,
         tuple(got), "x_sum",
     )
-    two_last = all_to_all(two.reshape(NZ * NY, -1, width), ("z", "grp"))
-    grad_w_two = jnp.sum(two_last.astype(F32), axis=0)
+    grad_w_two = jnp.sum(all_to_all(two, ("z", "grp")), axis=0)
     got = [total] + [shift(total, "grp", NY, e) for e in range(1, NY)]
     grad_w_one, grad_b_one = call(
         y_sum_kernel,

time: 252 us -> 254 us (level)
  starting transfers between devices: 62 us -> 66.8 us
    all_to_all x4, starting transfers between devices: 41.8 us -> 46.6 us  [all_to_all(): return lax.all_to_all(value, axes, split_axis=0, concat_axis=0, tiled=True)]
    pallas_call x11 -> x10, Pallas kernels: 80.5 us -> 78.4 us  [call(): pl.pallas_call(body, out_shape=outs, in_specs=ins, out_specs=jax.tree.map...]
  transfers between devices with their start and end apart: 21 -> 21, of which waited for: 11 -> 10; matrix products, arithmetic and copies ran while one was open for 4% -> 4% of each run, Pallas kernels for 26% -> 25%
where the time goes in v4:
time: 254 us; the launch traced here: 253 us
  Pallas kernels  78.4 us (31%)
  starting transfers between devices  66.8 us (26%)
  waiting for transfers between devices  40.6 us (16%)
  blocking collectives  35.4 us (14%)
  local copies, waits for them, and re-layouts  16.1 us (6%)
  between operations  14.3 us (6%)
    pallas_call x10, Pallas kernels, call(): pl.pallas_call(body, out_shape=outs, in_specs=ins, out_specs=jax.tree.map...  78.4 us
    all_to_all x4, starting transfers between devices, all_to_all(): return lax.all_to_all(value, axes, split_axis=0, concat_axis=0, tiled=True)  46.6 us
    ppermute x15, waiting for transfers between devices, shift(): lax.ppermute(value, axis, [(s, (s + by) % size) for s in range(size)])  37.6 us
    all_to_all x1, blocking collectives, all_to_all(): return lax.all_to_all(value, axes, split_axis=0, concat_axis=0, tiled=True)  35.4 us
    ppermute x15, starting transfers between devices, shift(): lax.ppermute(value, axis, [(s, (s + by) % size) for s in range(size)])  20.2 us
    unnamed x46, local copies, waits for them, and re-layouts  7.06 us
  transfers between devices with their start and end apart: 21, of which 10 were waited for; matrix products, arithmetic and copies ran while one was open for 4% of the time, Pallas kernels for 25%

profile of v4, /device:TPU:2, one launch (start us, length us, event | category | flops | bytes accessed | tf_op | source)
XLA Modules:
  0.0 252.9 jit_solution(17783876155654346854)
XLA Ops:
  9.3 3.4 %table_grad.1 = (bf16[512,512]{1,0:T(8,128)(2,1)}, f32[128,512]{1,0:T(8,128)}, bf16[512,128]{1,0:T(8,128)(2,1)}) custom-call(bf16[128,512]{1,0:T(8,128)(2,1)} %bitcast.46, bf16[1024,512]{1,0:T(8,128)(2,1)} %w_two.3, s32[1,25,128]{2,1,0:T(8,128)} %copy.17.slot, s32[1,128]{1,0:T(1,128)} %deg_row.3), custom_call_target="tpu_custom_call" | custom-call | bytes 10800000 | tf_op jit(solution)/shard_map/table_grad/pallas_call | solution.py:37
  14.7 14.8 %all-to-all-start = ((bf16[256,2,512]{2,1,0:T(2,128)(2,1)}), bf16[256,2,512]{2,1,0:T(2,128)(2,1)S(1)}, u32[]{:S(2)}, u32[]{:S(2)}) async-start(bf16[256,2,512]{2,1,0:T(2,128)(2,1)} %reshape.42), calls=%async_computation | async-start | bytes 1048576 | tf_op jit(solution)/shard_map/all_to_all | solution.py:258
  32.2 22.1 %mean_first.1 = (bf16[32,128,128]{2,1,0:T(8,128)(2,1)}, bf16[32,128,128]{2,1,0:T(8,128)(2,1)}, f32[8192,128]{1,0:T(8,128)}) custom-call(s32[3]{0:T(128)} %pad_add_fusion.refs_0_.meta, s32[40960]{0:T(1024)} %reshape.41.refs_1_.refs_0_, bf16[64,8192]{1,0:T(8,128)(2,1)} %bitcast.42, bf16[64,8192]{1,0:T(8,128)(2,1)} %copy-done.6, ...), custom_call_target="tpu_custom_call" | custom-call | bytes 73296000 | tf_op jit(solution)/shard_map/mean_first/pallas_call | solution.py:37
  54.3 10.9 %all-to-all-start.2 = ((bf16[32,128,128]{2,1,0:T(8,128)(2,1)}), bf16[32,128,128]{2,1,0:T(8,128)(2,1)S(1)}, u32[]{:S(2)}, u32[]{:S(2)}) async-start(bf16[32,128,128]{2,1,0:T(8,128)(2,1)} %get-tuple-element.45), calls=%async_computation.2 | async-start | bytes 2097152 | tf_op jit(solution)/shard_map/all_to_all | solution.py:258
  68.6 2.4 collective-permute-start.3
  72.0 27.6 %mean_last.1 = bf16[32,128,128]{2,1,0:T(8,128)(2,1)} custom-call(s32[40960]{0:T(1024)} %reshape.41.refs_1_.refs_0_, f32[8192,128]{1,0:T(8,128)} %get-tuple-element.43.refs_1_, bf16[32,128,128]{2,1,0:T(8,128)(2,1)} %get-tuple-element.44.refs_2_, bf16[512,512]{1,0:T(8,128)(2,1)} %reshape.43.refs_3_.returned), custom_call_target="tpu_custom_call", output_to_operand_aliasing={{}: (2, {})} | custom-call | bytes 92160000 | tf_op jit(solution)/shard_map/mean_last/pallas_call | solution.py:37
  100.5 13.2 %all-to-all-start.1 = ((bf16[32,128,128]{2,1,0:T(8,128)(2,1)}), bf16[32,128,128]{2,1,0:T(8,128)(2,1)S(1)}, u32[]{:S(2)}, u32[]{:S(2)}) async-start(bf16[32,128,128]{2,1,0:T(8,128)(2,1)} %mean_last.1), calls=%async_computation.1 | async-start | bytes 2097152 | tf_op jit(solution)/shard_map/all_to_all | solution.py:258
  117.1 2.4 collective-permute-start.6
  120.5 4.5 %self_part.1 = f32[128,512]{1,0:T(8,128)} custom-call(bf16[32,128,128]{2,1,0:T(8,128)(2,1)} %copy-done.2, bf16[64,2,64,512]{3,2,1,0:T(8,128)(2,1)} %bitcast.37), custom_call_target="tpu_custom_call" | custom-call | bytes 14400000 | tf_op jit(solution)/shard_map/self_part/pallas_call | solution.py:37
  124.9 7.6 %collective-permute-done.4.refs_5_ = bf16[8,128,128]{2,1,0:T(8,128)(2,1)S(1)} collective-permute-done((bf16[8,128,128]{2,1,0:T(8,128)(2,1)}, bf16[8,128,128]{2,1,0:T(8,128)(2,1)S(1)}, u32[]{:S(2)}, u32[]{:S(2)}) %collective-permute-start.4) | collective-permute-done | bytes 262176 | tf_op jit(solution)/shard_map/ppermute | solution.py:59
  132.6 6.7 %collective-permute-done.6.refs_7_ = bf16[8,128,128]{2,1,0:T(8,128)(2,1)S(1)} collective-permute-done((bf16[8,128,128]{2,1,0:T(8,128)(2,1)}, bf16[8,128,128]{2,1,0:T(8,128)(2,1)S(1)}, u32[]{:S(2)}, u32[]{:S(2)}) %collective-permute-start.6) | collective-permute-done | bytes 262176 | tf_op jit(solution)/shard_map/ppermute | solution.py:59
  140.2 5.5 %node_update.1 = (bf16[128,512]{1,0:T(8,128)(2,1)}, bf16[128,512]{1,0:T(8,128)(2,1)}, bf16[512,512]{1,0:T(8,128)(2,1)}) custom-call(bf16[32,128,128]{2,1,0:T(8,128)(2,1)} %copy-done.3, bf16[64,2,64,512]{3,2,1,0:T(8,128)(2,1)} %bitcast.38, f32[128,512]{1,0:T(8,128)} %self_part.1, f32[1,512]{1,0:T(1,128)} %bitcast.49, f32[128,512]{1,0:T(8,128)} %get-tuple-element.52.d_self, ...), custom_call_target="tpu_custom_call" | custom-call | bytes 14400000 | tf_op jit(solution)/shard_map/node_update/pallas_call | solution.py:37
  147.0 35.4 %all_to_all.25 = bf16[256,2,512]{2,1,0:T(2,128)(2,1)S(1)} all-to-all(bf16[256,2,512]{2,1,0:T(2,128)(2,1)S(1)} %reshape.48), channel_id=1, replica_groups=mesh['x'=4,'z'=8,'core'=2,'grp'=4] {'x','z','core','grp'}, dimensions={0} | all-to-all | bytes 1048576 | tf_op jit(solution)/shard_map/all_to_all | solution.py:258
  183.4 3.6 %layer_two.1 = (bf16[128,512]{1,0:T(8,128)(2,1)}, f32[32,16,512]{2,1,0:T(8,128)}, bf16[32,16,512]{2,1,0:T(8,128)(2,1)}) custom-call(s32[3]{0:T(128)} %pad_add_fusion.refs_0_.meta, bf16[512,512]{1,0:T(8,128)(2,1)} %reshape.49.table, bf16[512,128]{1,0:T(8,128)(2,1)} %get-tuple-element.54.counts, s32[1,128]{1,0:T(1,128)} %deg_row.3, ...), custom_call_target="tpu_custom_call" | custom-call | bytes 10800000 | tf_op jit(solution)/shard_map/layer_two/pallas_call | solution.py:37
  188.8 4.6 %weight_grad.1 = (f32[4,144,512]{2,1,0:T(8,128)}, f32[4,144,512]{2,1,0:T(8,128)}) custom-call(s32[3]{0:T(128)} %pad_add_fusion.refs_0_.meta, bf16[8,128,128]{2,1,0:T(8,128)(2,1)} %get-tuple-element.57.refs_0_, bf16[8,128,128]{2,1,0:T(8,128)(2,1)} %copy-done.11, bf16[8,128,128]{2,1,0:T(8,128)(2,1)} %copy-done.12, bf16[8,128,128]{2,1,0:T(8,128)(2,1)} %copy-done.13, ...), custom_call_target="tpu_custom_call" | custom-call | bytes 54000000 | tf_op jit(solution)/shard_map/weight_grad/pallas_call | solution.py:37
  194.0 3.1 %collective-permute-done.8 = bf16[32,16,512]{2,1,0:T(8,128)(2,1)S(1)} collective-permute-done((bf16[32,16,512]{2,1,0:T(8,128)(2,1)S(1)}, bf16[32,16,512]{2,1,0:T(8,128)(2,1)S(1)}, u32[]{:S(2)}, u32[]{:S(2)}) %collective-permute-start.8) | collective-permute-done | bytes 524320 | tf_op jit(solution)/shard_map/ppermute | solution.py:59
  198.3 3.2 %core_sum.1 = (bf16[272,512]{1,0:T(8,128)(2,1)}, bf16[272,512]{1,0:T(8,128)(2,1)}, bf16[272,512]{1,0:T(8,128)(2,1)}, bf16[272,512]{1,0:T(8,128)(2,1)}) custom-call(s32[3]{0:T(128)} %pad_add_fusion.refs_0_.meta, f32[4,144,512]{2,1,0:T(8,128)} %get-tuple-element.68.own, f32[4,144,512]{2,1,0:T(8,128)} %copy-done.5, f32[4,128,512]{2,1,0:T(8,128)} %bitcast.44, ...), custom_call_target="tpu_custom_call" | custom-call | bytes 7200000 | tf_op jit(solution)/shard_map/core_sum/pallas_call | solution.py:37
  201.5 2.1 collective-permute-start.10
  205.6 7.2 %collective-permute-done.10.p2 = bf16[272,512]{1,0:T(8,128)(2,1)S(1)} collective-permute-done((bf16[272,512]{1,0:T(8,128)(2,1)}, bf16[272,512]{1,0:T(8,128)(2,1)S(1)}, u32[]{:S(2)}, u32[]{:S(2)}) %collective-permute-start.10) | collective-permute-done | bytes 278560 | tf_op jit(solution)/shard_map/ppermute | solution.py:59
  212.8 5.1 %collective-permute-done.11.p3 = bf16[272,512]{1,0:T(8,128)(2,1)S(1)} collective-permute-done((bf16[272,512]{1,0:T(8,128)(2,1)}, bf16[272,512]{1,0:T(8,128)(2,1)S(1)}, u32[]{:S(2)}, u32[]{:S(2)}) %collective-permute-start.11) | collective-permute-done | bytes 278560 | tf_op jit(solution)/shard_map/ppermute | solution.py:59
  220.8 7.7 %all-to-all-start.4 = ((f32[32,4,512]{2,1,0:T(4,128)}), f32[32,4,512]{2,1,0:T(4,128)S(1)}, u32[]{:S(2)}, u32[]{:S(2)}) async-start(f32[32,4,512]{2,1,0:T(4,128)} %get-tuple-element.79), calls=%async_computation.4 | async-start | bytes 524288 | tf_op jit(solution)/shard_map/all_to_all | solution.py:258
  230.3 2.7 %collective-permute-start.13 = (bf16[144,512]{1,0:T(8,128)(2,1)}, bf16[144,512]{1,0:T(8,128)(2,1)S(1)}, u32[]{:S(2)}, u32[]{:S(2)}) collective-permute-start(bf16[144,512]{1,0:T(8,128)(2,1)} %get-tuple-element.76.p0), channel_id=1, source_target_pairs={{0,2},{1,3},{2,0},{3,1},{4,6},{5,7},{6,4},{7,5},{8,10},{9,11},{10,... | collective-permute-start | bytes 442376 | tf_op jit(solution)/shard_map/ppermute | solution.py:59
  234.5 3.4 %collective-permute-done.12.p1 = bf16[144,512]{1,0:T(8,128)(2,1)S(1)} collective-permute-done((bf16[144,512]{1,0:T(8,128)(2,1)}, bf16[144,512]{1,0:T(8,128)(2,1)S(1)}, u32[]{:S(2)}, u32[]{:S(2)}) %collective-permute-start.12) | collective-permute-done | bytes 147488 | tf_op jit(solution)/shard_map/ppermute | solution.py:59
  237.8 4.4 %collective-permute-done.13.p2 = bf16[144,512]{1,0:T(8,128)(2,1)S(1)} collective-permute-done((bf16[144,512]{1,0:T(8,128)(2,1)}, bf16[144,512]{1,0:T(8,128)(2,1)S(1)}, u32[]{:S(2)}, u32[]{:S(2)}) %collective-permute-start.13) | collective-permute-done | bytes 147488 | tf_op jit(solution)/shard_map/ppermute | solution.py:59
  (89 shorter events, 35.1 us)
Async XLA Ops:
  7.2 22.4 %copy-start = (s32[1,10,8192]{2,0,1:T(1,128)S(1)}, s32[1,10,8192]{2,0,1:T(1,128)}, u32[]{:S(2)}) copy-start(s32[1,10,8192]{2,0,1:T(1,128)} %param.10) | copy-start | bytes 983044
  7.2 113.3 %all-gather.3.cloned.1.call-start = ((), (), s32[]{:S(2)}) async-start(), calls=%async_computation.5 | async-start | bytes 8519680 | tf_op jit(solution)/shard_map/all_gather | solution.py:275
  7.9 23.2 %collective-permute-start = (bf16[64,8192]{1,0:T(8,128)(2,1)}, bf16[64,8192]{1,0:T(8,128)(2,1)S(1)}, u32[]{:S(2)}, u32[]{:S(2)}) collective-permute-start(bf16[64,8192]{1,0:T(8,128)(2,1)} %bitcast.41), channel_id=1, source_target_pairs={{0,4},{4,0},{1,5},{5,1},{2,6},{6,2},{3,7},{7,3},{8,12},{12,8},{9,1... | collective-permute-start | bytes 3145736 | tf_op jit(solution)/shard_map/ppermute | solution.py:59
  14.7 39.6 %all-to-all-start = ((bf16[256,2,512]{2,1,0:T(2,128)(2,1)}), bf16[256,2,512]{2,1,0:T(2,128)(2,1)S(1)}, u32[]{:S(2)}, u32[]{:S(2)}) async-start(bf16[256,2,512]{2,1,0:T(2,128)(2,1)} %reshape.42), calls=%async_computation | async-start | bytes 1048576 | tf_op jit(solution)/shard_map/all_to_all | solution.py:258
  54.3 45.8 %all-to-all-start.2 = ((bf16[32,128,128]{2,1,0:T(8,128)(2,1)}), bf16[32,128,128]{2,1,0:T(8,128)(2,1)S(1)}, u32[]{:S(2)}, u32[]{:S(2)}) async-start(bf16[32,128,128]{2,1,0:T(8,128)(2,1)} %get-tuple-element.45), calls=%async_computation.2 | async-start | bytes 2097152 | tf_op jit(solution)/shard_map/all_to_all | solution.py:258
  66.3 33.4 %collective-permute-start.1 = (bf16[8,128,128]{2,1,0:T(8,128)(2,1)}, bf16[8,128,128]{2,1,0:T(8,128)(2,1)S(1)}, u32[]{:S(2)}, u32[]{:S(2)}) collective-permute-start(bf16[8,128,128]{2,1,0:T(8,128)(2,1)} %get-tuple-element.86), channel_id=1, source_target_pairs={{0,64},{64,128},{128,192},{192,0},{1,65},{65,129},{129,193},{193,1... | collective-permute-start | bytes 786440 | tf_op jit(solution)/shard_map/ppermute | solution.py:59
  67.7 31.9 %collective-permute-start.2 = (bf16[8,128,128]{2,1,0:T(8,128)(2,1)}, bf16[8,128,128]{2,1,0:T(8,128)(2,1)S(1)}, u32[]{:S(2)}, u32[]{:S(2)}) collective-permute-start(bf16[8,128,128]{2,1,0:T(8,128)(2,1)} %get-tuple-element.85), channel_id=1, source_target_pairs={{0,128},{64,192},{128,0},{192,64},{1,129},{65,193},{129,1},{193,65... | collective-permute-start | bytes 786440 | tf_op jit(solution)/shard_map/ppermute | solution.py:59
  68.6 31.1 %collective-permute-start.3 = (bf16[8,128,128]{2,1,0:T(8,128)(2,1)}, bf16[8,128,128]{2,1,0:T(8,128)(2,1)S(1)}, u32[]{:S(2)}, u32[]{:S(2)}) collective-permute-start(bf16[8,128,128]{2,1,0:T(8,128)(2,1)} %get-tuple-element.84), channel_id=1, source_target_pairs={{0,192},{64,0},{128,64},{192,128},{1,193},{65,1},{129,65},{193,129... | collective-permute-start | bytes 786440 | tf_op jit(solution)/shard_map/ppermute | solution.py:59
  99.6 14.2 %copy-start.1 = (bf16[32,128,128]{2,1,0:T(8,128)(2,1)S(1)}, bf16[32,128,128]{2,1,0:T(8,128)(2,1)}, u32[]{:S(2)}) copy-start(bf16[32,128,128]{2,1,0:T(8,128)(2,1)} %mean_last.1) | copy-start | bytes 3145732
  100.1 14.7 %copy-start.2 = (bf16[32,128,128]{2,1,0:T(8,128)(2,1)}, bf16[32,128,128]{2,1,0:T(8,128)(2,1)S(1)}, u32[]{:S(2)}) copy-start(bf16[32,128,128]{2,1,0:T(8,128)(2,1)S(1)} %all-to-all-done.2.left) | copy-start | bytes 3145732
  100.5 38.7 %all-to-all-start.1 = ((bf16[32,128,128]{2,1,0:T(8,128)(2,1)}), bf16[32,128,128]{2,1,0:T(8,128)(2,1)S(1)}, u32[]{:S(2)}, u32[]{:S(2)}) async-start(bf16[32,128,128]{2,1,0:T(8,128)(2,1)} %mean_last.1), calls=%async_computation.1 | async-start | bytes 2097152 | tf_op jit(solution)/shard_map/all_to_all | solution.py:258
  113.7 75.1 %all-gather.5.cloned.1.call-start = ((), (), s32[]{:S(2)}) async-start(), calls=%async_computation.6 | async-start | bytes 1179648 | tf_op jit(solution)/shard_map/all_gather | solution.py:358
  114.8 17.7 %collective-permute-start.4 = (bf16[8,128,128]{2,1,0:T(8,128)(2,1)}, bf16[8,128,128]{2,1,0:T(8,128)(2,1)S(1)}, u32[]{:S(2)}, u32[]{:S(2)}) collective-permute-start(bf16[8,128,128]{2,1,0:T(8,128)(2,1)} %get-tuple-element.82), channel_id=1, source_target_pairs={{0,64},{64,128},{128,192},{192,0},{1,65},{65,129},{129,193},{193,1... | collective-permute-start | bytes 786440 | tf_op jit(solution)/shard_map/ppermute | solution.py:59
  116.3 16.3 %collective-permute-start.5 = (bf16[8,128,128]{2,1,0:T(8,128)(2,1)}, bf16[8,128,128]{2,1,0:T(8,128)(2,1)S(1)}, u32[]{:S(2)}, u32[]{:S(2)}) collective-permute-start(bf16[8,128,128]{2,1,0:T(8,128)(2,1)} %get-tuple-element.81), channel_id=1, source_target_pairs={{0,128},{64,192},{128,0},{192,64},{1,129},{65,193},{129,1},{193,65... | collective-permute-start | bytes 786440 | tf_op jit(solution)/shard_map/ppermute | solution.py:59
  117.1 22.1 %collective-permute-start.6 = (bf16[8,128,128]{2,1,0:T(8,128)(2,1)}, bf16[8,128,128]{2,1,0:T(8,128)(2,1)S(1)}, u32[]{:S(2)}, u32[]{:S(2)}) collective-permute-start(bf16[8,128,128]{2,1,0:T(8,128)(2,1)} %get-tuple-element.80), channel_id=1, source_target_pairs={{0,192},{64,0},{128,64},{192,128},{1,193},{65,1},{129,65},{193,129... | collective-permute-start | bytes 786440 | tf_op jit(solution)/shard_map/ppermute | solution.py:59
  193.5 3.8 %collective-permute-start.7 = (f32[4,144,512]{2,1,0:T(8,128)}, f32[4,144,512]{2,1,0:T(8,128)S(1)}, u32[]{:S(2)}, u32[]{:S(2)}) collective-permute-start(f32[4,144,512]{2,1,0:T(8,128)} %get-tuple-element.69), channel_id=1, source_target_pairs={{0,4},{4,0},{1,5},{5,1},{2,6},{6,2},{3,7},{7,3},{8,12},{12,8},{9,1... | collective-permute-start | bytes 3538952 | tf_op jit(solution)/shard_map/ppermute | solution.py:59
  193.5 3.6 %collective-permute-start.8 = (bf16[32,16,512]{2,1,0:T(8,128)(2,1)S(1)}, bf16[32,16,512]{2,1,0:T(8,128)(2,1)S(1)}, u32[]{:S(2)}, u32[]{:S(2)}) collective-permute-start(bf16[32,16,512]{2,1,0:T(8,128)(2,1)S(1)} %copy-done.21), channel_id=1, source_target_pairs={{0,4},{4,0},{1,5},{5,1},{2,6},{6,2},{3,7},{7,3},{8,12},{12,8},{9,1... | collective-permute-start | bytes 1572872 | tf_op jit(solution)/shard_map/ppermute | solution.py:59
  201.5 11.3 %collective-permute-start.10 = (bf16[272,512]{1,0:T(8,128)(2,1)}, bf16[272,512]{1,0:T(8,128)(2,1)S(1)}, u32[]{:S(2)}, u32[]{:S(2)}) collective-permute-start(bf16[272,512]{1,0:T(8,128)(2,1)} %get-tuple-element.74), channel_id=1, source_target_pairs={{0,128},{64,192},{128,0},{192,64},{1,129},{65,193},{129,1},{193,65... | collective-permute-start | bytes 835592 | tf_op jit(solution)/shard_map/ppermute | solution.py:59
  203.6 14.3 %collective-permute-start.11 = (bf16[272,512]{1,0:T(8,128)(2,1)}, bf16[272,512]{1,0:T(8,128)(2,1)S(1)}, u32[]{:S(2)}, u32[]{:S(2)}) collective-permute-start(bf16[272,512]{1,0:T(8,128)(2,1)} %get-tuple-element.75), channel_id=1, source_target_pairs={{0,192},{64,0},{128,64},{192,128},{1,193},{65,1},{129,65},{193,129... | collective-permute-start | bytes 835592 | tf_op jit(solution)/shard_map/ppermute | solution.py:59
  204.9 13.0 %collective-permute-start.9 = (bf16[272,512]{1,0:T(8,128)(2,1)}, bf16[272,512]{1,0:T(8,128)(2,1)S(1)}, u32[]{:S(2)}, u32[]{:S(2)}) collective-permute-start(bf16[272,512]{1,0:T(8,128)(2,1)} %get-tuple-element.73), channel_id=1, source_target_pairs={{0,64},{64,128},{128,192},{192,0},{1,65},{65,129},{129,193},{193,1... | collective-permute-start | bytes 835592 | tf_op jit(solution)/shard_map/ppermute | solution.py:59
  220.8 24.6 %all-to-all-start.4 = ((f32[32,4,512]{2,1,0:T(4,128)}), f32[32,4,512]{2,1,0:T(4,128)S(1)}, u32[]{:S(2)}, u32[]{:S(2)}) async-start(f32[32,4,512]{2,1,0:T(4,128)} %get-tuple-element.79), calls=%async_computation.4 | async-start | bytes 524288 | tf_op jit(solution)/shard_map/all_to_all | solution.py:258
  228.5 9.4 %collective-permute-start.12 = (bf16[144,512]{1,0:T(8,128)(2,1)}, bf16[144,512]{1,0:T(8,128)(2,1)S(1)}, u32[]{:S(2)}, u32[]{:S(2)}) collective-permute-start(bf16[144,512]{1,0:T(8,128)(2,1)} %get-tuple-element.76.p0), channel_id=1, source_target_pairs={{0,1},{1,2},{2,3},{3,0},{4,5},{5,6},{6,7},{7,4},{8,9},{9,10},{10,1... | collective-permute-start | bytes 442376 | tf_op jit(solution)/shard_map/ppermute | solution.py:59
  230.3 11.9 %collective-permute-start.13 = (bf16[144,512]{1,0:T(8,128)(2,1)}, bf16[144,512]{1,0:T(8,128)(2,1)S(1)}, u32[]{:S(2)}, u32[]{:S(2)}) collective-permute-start(bf16[144,512]{1,0:T(8,128)(2,1)} %get-tuple-element.76.p0), channel_id=1, source_target_pairs={{0,2},{1,3},{2,0},{3,1},{4,6},{5,7},{6,4},{7,5},{8,10},{9,11},{10,... | collective-permute-start | bytes 442376 | tf_op jit(solution)/shard_map/ppermute | solution.py:59
  233.0 9.2 %collective-permute-start.14 = (bf16[144,512]{1,0:T(8,128)(2,1)}, bf16[144,512]{1,0:T(8,128)(2,1)S(1)}, u32[]{:S(2)}, u32[]{:S(2)}) collective-permute-start(bf16[144,512]{1,0:T(8,128)(2,1)} %get-tuple-element.76.p0), channel_id=1, source_target_pairs={{0,3},{1,0},{2,1},{3,2},{4,7},{5,4},{6,5},{7,6},{8,11},{9,8},{10,9... | collective-permute-start | bytes 442376 | tf_op jit(solution)/shard_map/ppermute | solution.py:59
  (19 other events, 72.8 us)
Sparse Core Ops, SparseCore 0:
  10.8 107.0 all-gather.2
  145.9 42.9 all-gather.4

commit v5 on v4

--- a/solution.py
+++ b/solution.py
@@ -11,7 +11,7 @@
 CHIPS = NX * NZ
 STEPS = 4
 MEAN_STEPS = 8
-FIRST_MEANS = 3
+FIRST_MEANS = 2
 FEAT = ("x", "z", "core")
 CHIP = ("x", "z")
 ALL = ("x", "z", "core", "grp")

time: 254 us -> 249 us (0.980)
  starting transfers between devices: 66.8 us -> 60.5 us
    ppermute x15, waiting for transfers between devices: 37.6 us -> 28.1 us  [shift(): lax.ppermute(value, axis, [(s, (s + by) % size) for s in range(size)])]
    all_gather x1, waiting for transfers between devices: 0.01 us -> 8.16 us  [on_device(): w_all = lax.all_gather(w_one.reshape(-1, width), FEAT, axis=0, tiled=True)]
    all_to_all x4, starting transfers between devices: 46.6 us -> 40.3 us  [all_to_all(): return lax.all_to_all(value, axes, split_axis=0, concat_axis=0, tiled=True)]
    all_to_all x4, waiting for transfers between devices: 0.48 us -> 3.53 us  [all_to_all(): return lax.all_to_all(value, axes, split_axis=0, concat_axis=0, tiled=True)]
  transfers between devices with their start and end apart: 21 -> 21, of which waited for: 10 -> 11; matrix products, arithmetic and copies ran while one was open for 4% -> 4% of each run, Pallas kernels for 25% -> 25%
where the time goes in v5:
time: 249 us; the launch traced here: 248 us
  Pallas kernels  78.4 us (31%)
  starting transfers between devices  60.5 us (24%)
  waiting for transfers between devices  42.3 us (17%)
  blocking collectives  35.1 us (14%)
  local copies, waits for them, and re-layouts  16.5 us (7%)
  between operations  14.3 us (6%)
    pallas_call x10, Pallas kernels, call(): pl.pallas_call(body, out_shape=outs, in_specs=ins, out_specs=jax.tree.map...  78.4 us
    all_to_all x4, starting transfers between devices, all_to_all(): return lax.all_to_all(value, axes, split_axis=0, concat_axis=0, tiled=True)  40.3 us
    all_to_all x1, blocking collectives, all_to_all(): return lax.all_to_all(value, axes, split_axis=0, concat_axis=0, tiled=True)  35.1 us
    ppermute x15, waiting for transfers between devices, shift(): lax.ppermute(value, axis, [(s, (s + by) % size) for s in range(size)])  28.1 us
    ppermute x15, starting transfers between devices, shift(): lax.ppermute(value, axis, [(s, (s + by) % size) for s in range(size)])  20.2 us
    all_gather x1, waiting for transfers between devices, on_device(): w_all = lax.all_gather(w_one.reshape(-1, width), FEAT, axis=0, tiled=True)  8.16 us
    unnamed x46, local copies, waits for them, and re-layouts  7.48 us
  transfers between devices with their start and end apart: 21, of which 11 were waited for; matrix products, arithmetic and copies ran while one was open for 4% of the time, Pallas kernels for 25%

profile of v5, /device:TPU:2, one launch (start us, length us, event | category | flops | bytes accessed | tf_op | source)
XLA Modules:
  0.0 248.4 jit_solution(6453952346651006782)
XLA Ops:
  9.3 3.4 %table_grad.1 = (bf16[512,512]{1,0:T(8,128)(2,1)}, f32[128,512]{1,0:T(8,128)}, bf16[512,128]{1,0:T(8,128)(2,1)}) custom-call(bf16[128,512]{1,0:T(8,128)(2,1)} %bitcast.46, bf16[1024,512]{1,0:T(8,128)(2,1)} %w_two.3, s32[1,25,128]{2,1,0:T(8,128)} %copy.17.slot, s32[1,128]{1,0:T(1,128)} %deg_row.3), custom_call_target="tpu_custom_call" | custom-call | bytes 10800000 | tf_op jit(solution)/shard_map/table_grad/pallas_call | solution.py:37
  14.7 14.8 %all-to-all-start = ((bf16[256,2,512]{2,1,0:T(2,128)(2,1)}), bf16[256,2,512]{2,1,0:T(2,128)(2,1)S(1)}, u32[]{:S(2)}, u32[]{:S(2)}) async-start(bf16[256,2,512]{2,1,0:T(2,128)(2,1)} %reshape.42), calls=%async_computation | async-start | bytes 1048576 | tf_op jit(solution)/shard_map/all_to_all | solution.py:258
  32.2 17.4 %mean_first.1 = (bf16[32,128,128]{2,1,0:T(8,128)(2,1)}, bf16[32,128,128]{2,1,0:T(8,128)(2,1)}, f32[8192,128]{1,0:T(8,128)}) custom-call(s32[3]{0:T(128)} %pad_add_fusion.refs_0_.meta, s32[40960]{0:T(1024)} %reshape.41.refs_1_.refs_0_, bf16[64,8192]{1,0:T(8,128)(2,1)} %bitcast.42, bf16[64,8192]{1,0:T(8,128)(2,1)} %copy-done.6, ...), custom_call_target="tpu_custom_call" | custom-call | bytes 54864000 | tf_op jit(solution)/shard_map/mean_first/pallas_call | solution.py:37
  51.1 9.3 %all-to-all-start.2 = ((bf16[32,128,128]{2,1,0:T(8,128)(2,1)}), bf16[32,128,128]{2,1,0:T(8,128)(2,1)S(1)}, u32[]{:S(2)}, u32[]{:S(2)}) async-start(bf16[32,128,128]{2,1,0:T(8,128)(2,1)} %get-tuple-element.45), calls=%async_computation.2 | async-start | bytes 2097152 | tf_op jit(solution)/shard_map/all_to_all | solution.py:258
  63.8 2.4 collective-permute-start.3
  67.3 32.3 %mean_last.1 = bf16[32,128,128]{2,1,0:T(8,128)(2,1)} custom-call(s32[40960]{0:T(1024)} %reshape.41.refs_1_.refs_0_, f32[8192,128]{1,0:T(8,128)} %get-tuple-element.43.refs_1_, bf16[32,128,128]{2,1,0:T(8,128)(2,1)} %get-tuple-element.44.refs_2_, bf16[512,512]{1,0:T(8,128)(2,1)} %reshape.43.refs_3_.returned), custom_call_target="tpu_custom_call", output_to_operand_aliasing={{}: (2, {})} | custom-call | bytes 110592000 | tf_op jit(solution)/shard_map/mean_last/pallas_call | solution.py:37
  100.5 8.4 %all-to-all-start.1 = ((bf16[32,128,128]{2,1,0:T(8,128)(2,1)}), bf16[32,128,128]{2,1,0:T(8,128)(2,1)S(1)}, u32[]{:S(2)}, u32[]{:S(2)}) async-start(bf16[32,128,128]{2,1,0:T(8,128)(2,1)} %mean_last.1), calls=%async_computation.1 | async-start | bytes 2097152 | tf_op jit(solution)/shard_map/all_to_all | solution.py:258
  112.4 2.4 collective-permute-start.6
  115.7 8.2 %all-gather.3.cloned.1.call-done = bf16[8192,512]{1,0:T(8,128)(2,1)} async-done(((bf16[128,512]{1,0:T(8,128)(2,1)}), bf16[8192,512]{1,0:T(8,128)(2,1)}) %all-gather.3.cloned.1.call-update) | async-done | bytes 8388624 | tf_op jit(solution)/shard_map/all_gather | solution.py:275
  123.8 4.5 %self_part.1 = f32[128,512]{1,0:T(8,128)} custom-call(bf16[32,128,128]{2,1,0:T(8,128)(2,1)} %copy-done.2, bf16[64,2,64,512]{3,2,1,0:T(8,128)(2,1)} %bitcast.37), custom_call_target="tpu_custom_call" | custom-call | bytes 14400000 | tf_op jit(solution)/shard_map/self_part/pallas_call | solution.py:37
  128.3 4.8 %collective-permute-done.6.refs_7_ = bf16[8,128,128]{2,1,0:T(8,128)(2,1)S(1)} collective-permute-done((bf16[8,128,128]{2,1,0:T(8,128)(2,1)}, bf16[8,128,128]{2,1,0:T(8,128)(2,1)S(1)}, u32[]{:S(2)}, u32[]{:S(2)}) %collective-permute-start.6) | collective-permute-done | bytes 262176 | tf_op jit(solution)/shard_map/ppermute | solution.py:59
  136.1 5.5 %node_update.1 = (bf16[128,512]{1,0:T(8,128)(2,1)}, bf16[128,512]{1,0:T(8,128)(2,1)}, bf16[512,512]{1,0:T(8,128)(2,1)}) custom-call(bf16[32,128,128]{2,1,0:T(8,128)(2,1)} %copy-done.3, bf16[64,2,64,512]{3,2,1,0:T(8,128)(2,1)} %bitcast.38, f32[128,512]{1,0:T(8,128)} %self_part.1, f32[1,512]{1,0:T(1,128)} %bitcast.49, f32[128,512]{1,0:T(8,128)} %get-tuple-element.52.d_self, ...), custom_call_target="tpu_custom_call" | custom-call | bytes 14400000 | tf_op jit(solution)/shard_map/node_update/pallas_call | solution.py:37
  142.8 35.1 %all_to_all.25 = bf16[256,2,512]{2,1,0:T(2,128)(2,1)S(1)} all-to-all(bf16[256,2,512]{2,1,0:T(2,128)(2,1)S(1)} %reshape.48), channel_id=1, replica_groups=mesh['x'=4,'z'=8,'core'=2,'grp'=4] {'x','z','core','grp'}, dimensions={0} | all-to-all | bytes 1048576 | tf_op jit(solution)/shard_map/all_to_all | solution.py:258
  178.9 3.6 %layer_two.1 = (bf16[128,512]{1,0:T(8,128)(2,1)}, f32[32,16,512]{2,1,0:T(8,128)}, bf16[32,16,512]{2,1,0:T(8,128)(2,1)}) custom-call(s32[3]{0:T(128)} %pad_add_fusion.refs_0_.meta, bf16[512,512]{1,0:T(8,128)(2,1)} %reshape.49.table, bf16[512,128]{1,0:T(8,128)(2,1)} %get-tuple-element.54.counts, s32[1,128]{1,0:T(1,128)} %deg_row.3, ...), custom_call_target="tpu_custom_call" | custom-call | bytes 10800000 | tf_op jit(solution)/shard_map/layer_two/pallas_call | solution.py:37
  184.3 4.7 %weight_grad.1 = (f32[4,144,512]{2,1,0:T(8,128)}, f32[4,144,512]{2,1,0:T(8,128)}) custom-call(s32[3]{0:T(128)} %pad_add_fusion.refs_0_.meta, bf16[8,128,128]{2,1,0:T(8,128)(2,1)} %get-tuple-element.57.refs_0_, bf16[8,128,128]{2,1,0:T(8,128)(2,1)} %copy-done.11, bf16[8,128,128]{2,1,0:T(8,128)(2,1)} %copy-done.12, bf16[8,128,128]{2,1,0:T(8,128)(2,1)} %copy-done.13, ...), custom_call_target="tpu_custom_call" | custom-call | bytes 54000000 | tf_op jit(solution)/shard_map/weight_grad/pallas_call | solution.py:37
  189.5 3.1 %collective-permute-done.8 = bf16[32,16,512]{2,1,0:T(8,128)(2,1)S(1)} collective-permute-done((bf16[32,16,512]{2,1,0:T(8,128)(2,1)S(1)}, bf16[32,16,512]{2,1,0:T(8,128)(2,1)S(1)}, u32[]{:S(2)}, u32[]{:S(2)}) %collective-permute-start.8) | collective-permute-done | bytes 524320 | tf_op jit(solution)/shard_map/ppermute | solution.py:59
  193.8 3.2 %core_sum.1 = (bf16[272,512]{1,0:T(8,128)(2,1)}, bf16[272,512]{1,0:T(8,128)(2,1)}, bf16[272,512]{1,0:T(8,128)(2,1)}, bf16[272,512]{1,0:T(8,128)(2,1)}) custom-call(s32[3]{0:T(128)} %pad_add_fusion.refs_0_.meta, f32[4,144,512]{2,1,0:T(8,128)} %get-tuple-element.68.own, f32[4,144,512]{2,1,0:T(8,128)} %copy-done.5, f32[4,128,512]{2,1,0:T(8,128)} %bitcast.44, ...), custom_call_target="tpu_custom_call" | custom-call | bytes 7200000 | tf_op jit(solution)/shard_map/core_sum/pallas_call | solution.py:37
  197.0 2.1 collective-permute-start.10
  201.1 7.2 %collective-permute-done.10.p2 = bf16[272,512]{1,0:T(8,128)(2,1)S(1)} collective-permute-done((bf16[272,512]{1,0:T(8,128)(2,1)}, bf16[272,512]{1,0:T(8,128)(2,1)S(1)}, u32[]{:S(2)}, u32[]{:S(2)}) %collective-permute-start.10) | collective-permute-done | bytes 278560 | tf_op jit(solution)/shard_map/ppermute | solution.py:59
  208.3 5.1 %collective-permute-done.11.p3 = bf16[272,512]{1,0:T(8,128)(2,1)S(1)} collective-permute-done((bf16[272,512]{1,0:T(8,128)(2,1)}, bf16[272,512]{1,0:T(8,128)(2,1)S(1)}, u32[]{:S(2)}, u32[]{:S(2)}) %collective-permute-start.11) | collective-permute-done | bytes 278560 | tf_op jit(solution)/shard_map/ppermute | solution.py:59
  216.3 7.7 %all-to-all-start.4 = ((f32[32,4,512]{2,1,0:T(4,128)}), f32[32,4,512]{2,1,0:T(4,128)S(1)}, u32[]{:S(2)}, u32[]{:S(2)}) async-start(f32[32,4,512]{2,1,0:T(4,128)} %get-tuple-element.79), calls=%async_computation.4 | async-start | bytes 524288 | tf_op jit(solution)/shard_map/all_to_all | solution.py:258
  225.8 2.7 %collective-permute-start.13 = (bf16[144,512]{1,0:T(8,128)(2,1)}, bf16[144,512]{1,0:T(8,128)(2,1)S(1)}, u32[]{:S(2)}, u32[]{:S(2)}) collective-permute-start(bf16[144,512]{1,0:T(8,128)(2,1)} %get-tuple-element.76.p0), channel_id=1, source_target_pairs={{0,2},{1,3},{2,0},{3,1},{4,6},{5,7},{6,4},{7,5},{8,10},{9,11},{10,... | collective-permute-start | bytes 442376 | tf_op jit(solution)/shard_map/ppermute | solution.py:59
  230.0 3.4 %collective-permute-done.12.p1 = bf16[144,512]{1,0:T(8,128)(2,1)S(1)} collective-permute-done((bf16[144,512]{1,0:T(8,128)(2,1)}, bf16[144,512]{1,0:T(8,128)(2,1)S(1)}, u32[]{:S(2)}, u32[]{:S(2)}) %collective-permute-start.12) | collective-permute-done | bytes 147488 | tf_op jit(solution)/shard_map/ppermute | solution.py:59
  233.3 4.4 %collective-permute-done.13.p2 = bf16[144,512]{1,0:T(8,128)(2,1)S(1)} collective-permute-done((bf16[144,512]{1,0:T(8,128)(2,1)}, bf16[144,512]{1,0:T(8,128)(2,1)S(1)}, u32[]{:S(2)}, u32[]{:S(2)}) %collective-permute-start.13) | collective-permute-done | bytes 147488 | tf_op jit(solution)/shard_map/ppermute | solution.py:59
  (89 shorter events, 38.6 us)
Async XLA Ops:
  7.2 22.4 %copy-start = (s32[1,10,8192]{2,0,1:T(1,128)S(1)}, s32[1,10,8192]{2,0,1:T(1,128)}, u32[]{:S(2)}) copy-start(s32[1,10,8192]{2,0,1:T(1,128)} %param.10) | copy-start | bytes 983044
  7.2 116.7 %all-gather.3.cloned.1.call-start = ((), (), s32[]{:S(2)}) async-start(), calls=%async_computation.5 | async-start | bytes 8519680 | tf_op jit(solution)/shard_map/all_gather | solution.py:275
  7.9 23.2 %collective-permute-start = (bf16[64,8192]{1,0:T(8,128)(2,1)}, bf16[64,8192]{1,0:T(8,128)(2,1)S(1)}, u32[]{:S(2)}, u32[]{:S(2)}) collective-permute-start(bf16[64,8192]{1,0:T(8,128)(2,1)} %bitcast.41), channel_id=1, source_target_pairs={{0,4},{4,0},{1,5},{5,1},{2,6},{6,2},{3,7},{7,3},{8,12},{12,8},{9,1... | collective-permute-start | bytes 3145736 | tf_op jit(solution)/shard_map/ppermute | solution.py:59
  14.7 36.4 %all-to-all-start = ((bf16[256,2,512]{2,1,0:T(2,128)(2,1)}), bf16[256,2,512]{2,1,0:T(2,128)(2,1)S(1)}, u32[]{:S(2)}, u32[]{:S(2)}) async-start(bf16[256,2,512]{2,1,0:T(2,128)(2,1)} %reshape.42), calls=%async_computation | async-start | bytes 1048576 | tf_op jit(solution)/shard_map/all_to_all | solution.py:258
  51.1 48.6 %all-to-all-start.2 = ((bf16[32,128,128]{2,1,0:T(8,128)(2,1)}), bf16[32,128,128]{2,1,0:T(8,128)(2,1)S(1)}, u32[]{:S(2)}, u32[]{:S(2)}) async-start(bf16[32,128,128]{2,1,0:T(8,128)(2,1)} %get-tuple-element.45), calls=%async_computation.2 | async-start | bytes 2097152 | tf_op jit(solution)/shard_map/all_to_all | solution.py:258
  61.5 38.1 %collective-permute-start.1 = (bf16[8,128,128]{2,1,0:T(8,128)(2,1)}, bf16[8,128,128]{2,1,0:T(8,128)(2,1)S(1)}, u32[]{:S(2)}, u32[]{:S(2)}) collective-permute-start(bf16[8,128,128]{2,1,0:T(8,128)(2,1)} %get-tuple-element.86), channel_id=1, source_target_pairs={{0,64},{64,128},{128,192},{192,0},{1,65},{65,129},{129,193},{193,1... | collective-permute-start | bytes 786440 | tf_op jit(solution)/shard_map/ppermute | solution.py:59
  63.0 36.6 %collective-permute-start.2 = (bf16[8,128,128]{2,1,0:T(8,128)(2,1)}, bf16[8,128,128]{2,1,0:T(8,128)(2,1)S(1)}, u32[]{:S(2)}, u32[]{:S(2)}) collective-permute-start(bf16[8,128,128]{2,1,0:T(8,128)(2,1)} %get-tuple-element.85), channel_id=1, source_target_pairs={{0,128},{64,192},{128,0},{192,64},{1,129},{65,193},{129,1},{193,65... | collective-permute-start | bytes 786440 | tf_op jit(solution)/shard_map/ppermute | solution.py:59
  63.8 35.8 %collective-permute-start.3 = (bf16[8,128,128]{2,1,0:T(8,128)(2,1)}, bf16[8,128,128]{2,1,0:T(8,128)(2,1)S(1)}, u32[]{:S(2)}, u32[]{:S(2)}) collective-permute-start(bf16[8,128,128]{2,1,0:T(8,128)(2,1)} %get-tuple-element.84), channel_id=1, source_target_pairs={{0,192},{64,0},{128,64},{192,128},{1,193},{65,1},{129,65},{193,129... | collective-permute-start | bytes 786440 | tf_op jit(solution)/shard_map/ppermute | solution.py:59
  100.5 34.6 %all-to-all-start.1 = ((bf16[32,128,128]{2,1,0:T(8,128)(2,1)}), bf16[32,128,128]{2,1,0:T(8,128)(2,1)S(1)}, u32[]{:S(2)}, u32[]{:S(2)}) async-start(bf16[32,128,128]{2,1,0:T(8,128)(2,1)} %mean_last.1), calls=%async_computation.1 | async-start | bytes 2097152 | tf_op jit(solution)/shard_map/all_to_all | solution.py:258
  109.0 75.4 %all-gather.5.cloned.1.call-start = ((), (), s32[]{:S(2)}) async-start(), calls=%async_computation.6 | async-start | bytes 1179648 | tf_op jit(solution)/shard_map/all_gather | solution.py:358
  110.1 18.3 %collective-permute-start.4 = (bf16[8,128,128]{2,1,0:T(8,128)(2,1)}, bf16[8,128,128]{2,1,0:T(8,128)(2,1)S(1)}, u32[]{:S(2)}, u32[]{:S(2)}) collective-permute-start(bf16[8,128,128]{2,1,0:T(8,128)(2,1)} %get-tuple-element.82), channel_id=1, source_target_pairs={{0,64},{64,128},{128,192},{192,0},{1,65},{65,129},{129,193},{193,1... | collective-permute-start | bytes 786440 | tf_op jit(solution)/shard_map/ppermute | solution.py:59
  111.5 16.8 %collective-permute-start.5 = (bf16[8,128,128]{2,1,0:T(8,128)(2,1)}, bf16[8,128,128]{2,1,0:T(8,128)(2,1)S(1)}, u32[]{:S(2)}, u32[]{:S(2)}) collective-permute-start(bf16[8,128,128]{2,1,0:T(8,128)(2,1)} %get-tuple-element.81), channel_id=1, source_target_pairs={{0,128},{64,192},{128,0},{192,64},{1,129},{65,193},{129,1},{193,65... | collective-permute-start | bytes 786440 | tf_op jit(solution)/shard_map/ppermute | solution.py:59
  112.4 20.8 %collective-permute-start.6 = (bf16[8,128,128]{2,1,0:T(8,128)(2,1)}, bf16[8,128,128]{2,1,0:T(8,128)(2,1)S(1)}, u32[]{:S(2)}, u32[]{:S(2)}) collective-permute-start(bf16[8,128,128]{2,1,0:T(8,128)(2,1)} %get-tuple-element.80), channel_id=1, source_target_pairs={{0,192},{64,0},{128,64},{192,128},{1,193},{65,1},{129,65},{193,129... | collective-permute-start | bytes 786440 | tf_op jit(solution)/shard_map/ppermute | solution.py:59
  128.3 13.2 %copy-start.14 = (bf16[8,128,128]{2,1,0:T(8,128)(2,1)}, bf16[8,128,128]{2,1,0:T(8,128)(2,1)S(1)}, u32[]{:S(2)}) copy-start(bf16[8,128,128]{2,1,0:T(8,128)(2,1)S(1)} %collective-permute-done.4.refs_5_) | copy-start | bytes 786436
  128.3 13.2 %copy-start.15 = (bf16[8,128,128]{2,1,0:T(8,128)(2,1)}, bf16[8,128,128]{2,1,0:T(8,128)(2,1)S(1)}, u32[]{:S(2)}) copy-start(bf16[8,128,128]{2,1,0:T(8,128)(2,1)S(1)} %collective-permute-done.5.refs_6_) | copy-start | bytes 786436
  189.0 3.8 %collective-permute-start.7 = (f32[4,144,512]{2,1,0:T(8,128)}, f32[4,144,512]{2,1,0:T(8,128)S(1)}, u32[]{:S(2)}, u32[]{:S(2)}) collective-permute-start(f32[4,144,512]{2,1,0:T(8,128)} %get-tuple-element.69), channel_id=1, source_target_pairs={{0,4},{4,0},{1,5},{5,1},{2,6},{6,2},{3,7},{7,3},{8,12},{12,8},{9,1... | collective-permute-start | bytes 3538952 | tf_op jit(solution)/shard_map/ppermute | solution.py:59
  189.0 3.6 %collective-permute-start.8 = (bf16[32,16,512]{2,1,0:T(8,128)(2,1)S(1)}, bf16[32,16,512]{2,1,0:T(8,128)(2,1)S(1)}, u32[]{:S(2)}, u32[]{:S(2)}) collective-permute-start(bf16[32,16,512]{2,1,0:T(8,128)(2,1)S(1)} %copy-done.21), channel_id=1, source_target_pairs={{0,4},{4,0},{1,5},{5,1},{2,6},{6,2},{3,7},{7,3},{8,12},{12,8},{9,1... | collective-permute-start | bytes 1572872 | tf_op jit(solution)/shard_map/ppermute | solution.py:59
  197.0 11.3 %collective-permute-start.10 = (bf16[272,512]{1,0:T(8,128)(2,1)}, bf16[272,512]{1,0:T(8,128)(2,1)S(1)}, u32[]{:S(2)}, u32[]{:S(2)}) collective-permute-start(bf16[272,512]{1,0:T(8,128)(2,1)} %get-tuple-element.74), channel_id=1, source_target_pairs={{0,128},{64,192},{128,0},{192,64},{1,129},{65,193},{129,1},{193,65... | collective-permute-start | bytes 835592 | tf_op jit(solution)/shard_map/ppermute | solution.py:59
  199.1 14.3 %collective-permute-start.11 = (bf16[272,512]{1,0:T(8,128)(2,1)}, bf16[272,512]{1,0:T(8,128)(2,1)S(1)}, u32[]{:S(2)}, u32[]{:S(2)}) collective-permute-start(bf16[272,512]{1,0:T(8,128)(2,1)} %get-tuple-element.75), channel_id=1, source_target_pairs={{0,192},{64,0},{128,64},{192,128},{1,193},{65,1},{129,65},{193,129... | collective-permute-start | bytes 835592 | tf_op jit(solution)/shard_map/ppermute | solution.py:59
  200.4 13.0 %collective-permute-start.9 = (bf16[272,512]{1,0:T(8,128)(2,1)}, bf16[272,512]{1,0:T(8,128)(2,1)S(1)}, u32[]{:S(2)}, u32[]{:S(2)}) collective-permute-start(bf16[272,512]{1,0:T(8,128)(2,1)} %get-tuple-element.73), channel_id=1, source_target_pairs={{0,64},{64,128},{128,192},{192,0},{1,65},{65,129},{129,193},{193,1... | collective-permute-start | bytes 835592 | tf_op jit(solution)/shard_map/ppermute | solution.py:59
  216.3 24.6 %all-to-all-start.4 = ((f32[32,4,512]{2,1,0:T(4,128)}), f32[32,4,512]{2,1,0:T(4,128)S(1)}, u32[]{:S(2)}, u32[]{:S(2)}) async-start(f32[32,4,512]{2,1,0:T(4,128)} %get-tuple-element.79), calls=%async_computation.4 | async-start | bytes 524288 | tf_op jit(solution)/shard_map/all_to_all | solution.py:258
  224.0 9.4 %collective-permute-start.12 = (bf16[144,512]{1,0:T(8,128)(2,1)}, bf16[144,512]{1,0:T(8,128)(2,1)S(1)}, u32[]{:S(2)}, u32[]{:S(2)}) collective-permute-start(bf16[144,512]{1,0:T(8,128)(2,1)} %get-tuple-element.76.p0), channel_id=1, source_target_pairs={{0,1},{1,2},{2,3},{3,0},{4,5},{5,6},{6,7},{7,4},{8,9},{9,10},{10,1... | collective-permute-start | bytes 442376 | tf_op jit(solution)/shard_map/ppermute | solution.py:59
  225.8 11.9 %collective-permute-start.13 = (bf16[144,512]{1,0:T(8,128)(2,1)}, bf16[144,512]{1,0:T(8,128)(2,1)S(1)}, u32[]{:S(2)}, u32[]{:S(2)}) collective-permute-start(bf16[144,512]{1,0:T(8,128)(2,1)} %get-tuple-element.76.p0), channel_id=1, source_target_pairs={{0,2},{1,3},{2,0},{3,1},{4,6},{5,7},{6,4},{7,5},{8,10},{9,11},{10,... | collective-permute-start | bytes 442376 | tf_op jit(solution)/shard_map/ppermute | solution.py:59
  228.5 9.2 %collective-permute-start.14 = (bf16[144,512]{1,0:T(8,128)(2,1)}, bf16[144,512]{1,0:T(8,128)(2,1)S(1)}, u32[]{:S(2)}, u32[]{:S(2)}) collective-permute-start(bf16[144,512]{1,0:T(8,128)(2,1)} %get-tuple-element.76.p0), channel_id=1, source_target_pairs={{0,3},{1,0},{2,1},{3,2},{4,7},{5,4},{6,5},{7,6},{8,11},{9,8},{10,9... | collective-permute-start | bytes 442376 | tf_op jit(solution)/shard_map/ppermute | solution.py:59
  (19 other events, 68.2 us)
Sparse Core Ops, SparseCore 0:
  10.8 113.0 all-gather.2
  141.7 42.5 all-gather.4
